TPU v7x, 512 devices: a whole 4x8x8 slice. The times are simulated.
512 devices in a mesh: dp: 32 (over z, x), tensor: 16 (over y, core).
Axes of the slice: x: 4, y: 8, z: 8, core: 2. Of those that a mesh axis runs over, the one named last changes fastest.
Arguments:
- x_first: bfloat16 [256, 8192], P('dp', 'tensor'), may hold values from -64 to 64
- x_second: bfloat16 [256, 8192], P('dp', 'tensor'), may hold values from -64 to 64
- cache_keys: bfloat16 [256, 128, 1024], P('dp', 'tensor'), may hold values from -512 to 512
- cache_values: bfloat16 [256, 128, 1024], P('dp', 'tensor'), may hold values from -6 to 6
- ancestors: int32 [256], replicated, may hold values from 0 to 255, as said below
- attn_gain: float32 [8192], P('tensor'), may hold values from 0.1 to 1.9
- ffn_gain: float32 [8192], P('tensor'), may hold values from 0.1 to 1.9
- w_query: bfloat16 [8192, 8192], P('tensor', 'dp'), may hold values from -0.0625 to 0.0625
- w_keyval: bfloat16 [8192, 2048], P('tensor', 'dp'), may hold values from -0.0625 to 0.0625
- w_out: bfloat16 [8192, 8192], P('dp', 'tensor'), may hold values from -0.5 to 0.5
- w_gate: bfloat16 [8192, 14336], P('tensor', 'dp'), may hold values from -0.0625 to 0.0625
- w_up: bfloat16 [8192, 14336], P('tensor', 'dp'), may hold values from -0.0625 to 0.0625
- w_down: bfloat16 [14336, 8192], P('dp', 'tensor'), may hold values from -0.046875 to 0.046875
Outputs:
- attn_update: bfloat16 [2, 256, 8192], P(None, 'dp', 'tensor')
- ffn_update: bfloat16 [2, 256, 8192], P(None, 'dp', 'tensor')
Inputs may be any that keep to these rules, and one draw needn't show every extreme that they name: Particle p continues the cache of particle ancestors[p]. Among the 8 particles of one index of dp, at most 2 have ancestors in any one aligned block of 8 particles, and for every index of dp some block is named exactly 2 times.
All inputs are finite; a program needn't handle non-finite values.
Results may differ from a plain program's by a relative error of at most 0.04.
Values may be sent and summed in bfloat16 or wider, within the bound.
A program may use at most 64 MiB of HBM per device.

v0:
```python
import math

import jax
import jax.numpy as jnp
from jax import lax
from jax.sharding import PartitionSpec as P

KVH = 8
HD = 128
GROUP = 8


EPS = 1e-05
ROPE_BASE = 500000.0


def combined_all(x, axis, combine):
    everything = jax.tree.map(lambda part: lax.all_gather(part, axis), x)
    leading = jax.tree.map(lambda part: part[0], everything)

    def turn(k, so_far):
        return combine(so_far, jax.tree.map(lambda part: part[k], everything))

    return lax.fori_loop(1, lax.axis_size(axis), turn, leading)


def normalize(residual_in, gain):
    wide = residual_in.astype(jnp.float32)
    squares = lax.psum(jnp.sum(wide * wide, axis=1), "tensor")
    model_width = residual_in.shape[1] * lax.axis_size("tensor")
    return (wide * lax.rsqrt(squares[:, None] / model_width + EPS) * gain[None, :]).astype(
        jnp.bfloat16
    )


def project_rows(normed, weights):
    piece = lax.all_gather(normed, "dp", axis=0, tiled=True)
    return jnp.concatenate(
        [jnp.dot(piece, weight, preferred_element_type=jnp.float32) for weight in weights], axis=1
    )


def reduce_rows(left, weight):
    return lax.psum_scatter(
        jnp.dot(left, weight, preferred_element_type=jnp.float32).astype(jnp.bfloat16),
        "dp",
        scatter_dimension=0,
        tiled=True,
    ).astype(jnp.float32)


def rotate(tensor, position):
    half_width = tensor.shape[-1] // 2
    freq = jnp.power(
        jnp.float32(ROPE_BASE), -2.0 * jnp.arange(half_width, dtype=jnp.float32) / tensor.shape[-1]
    )
    angle = jnp.float32(position) * freq
    cosine = jnp.cos(angle)
    sine = jnp.sin(angle)
    first_half = tensor[..., :half_width]
    second_half = tensor[..., half_width:]
    return jnp.concatenate(
        [first_half * cosine - second_half * sine, second_half * cosine + first_half * sine],
        axis=-1,
    )


def project_step(residual_in, gain, w_query, w_keyval, position):
    normed = normalize(residual_in, gain)
    partial_value = project_rows(normed, (w_query, w_keyval))
    summed = lax.psum(partial_value, "tensor").astype(jnp.bfloat16)
    query_cols = w_query.shape[1]
    queries, keyvals = (
        lax.all_to_all(summed[:, :query_cols], "dp", split_axis=0, concat_axis=1, tiled=True),
        lax.all_to_all(summed[:, query_cols:], "dp", split_axis=0, concat_axis=1, tiled=True),
    )
    count = residual_in.shape[0]
    queries = rotate(queries.astype(jnp.float32).reshape(count, KVH, GROUP, HD), position).astype(
        jnp.bfloat16
    )
    keyvals = keyvals.reshape(count, 2, KVH, HD)
    new_keys = rotate(keyvals[:, 0].astype(jnp.float32), position).astype(jnp.bfloat16)
    return (queries, new_keys, keyvals[:, 1])


def partial_attention(queries, keys, values):
    scores = jnp.einsum("rkgd,rlkd->rkgl", queries, keys, preferred_element_type=jnp.float32) * (
        1.0 / math.sqrt(HD)
    )
    highest = jnp.max(scores, axis=-1)
    weights = jnp.exp(scores - highest[..., None])
    totals = jnp.sum(weights, axis=-1)
    mixed = jnp.einsum(
        "rkgl,rlkd->rkgd", weights, values.astype(jnp.float32), precision=lax.Precision.HIGHEST
    )
    return (highest, totals, mixed)


def combine(first, second):
    highest = jnp.maximum(first[0], second[0])
    first_scale = jnp.exp(first[0] - highest)
    second_scale = jnp.exp(second[0] - highest)
    totals = first[1] * first_scale + second[1] * second_scale
    mixed = first[2] * first_scale[..., None] + second[2] * second_scale[..., None]
    return (highest, totals, mixed)


def merge_positions(attn_state):
    return combined_all(attn_state, "tensor", combine)


def add_key(attn_state, queries, key_one, value_one):
    score = jnp.einsum("rkgd,rkd->rkg", queries, key_one, preferred_element_type=jnp.float32) * (
        1.0 / math.sqrt(HD)
    )
    spread = jnp.broadcast_to(value_one.astype(jnp.float32)[:, :, None, :], attn_state[2].shape)
    return combine(attn_state, (score, jnp.ones_like(score), spread))


def finish(attn_state):
    count = attn_state[2].shape[0]
    return (attn_state[2] / attn_state[1][..., None]).reshape(count, -1).astype(jnp.bfloat16)


def updates(residual_in, mixed, ffn_gain, w_out, w_gate, w_up, w_down):
    spread = lax.all_to_all(mixed, "dp", split_axis=1, concat_axis=0, tiled=True)
    attn_part = reduce_rows(spread, w_out).astype(jnp.bfloat16)
    hidden_in = (residual_in.astype(jnp.float32) + attn_part.astype(jnp.float32)).astype(
        jnp.bfloat16
    )
    normed = normalize(hidden_in, ffn_gain)
    partial_value = project_rows(normed, (w_gate, w_up))
    hidden_cols = w_gate.shape[1]
    summed = lax.psum(partial_value.astype(jnp.bfloat16), "tensor").astype(jnp.float32)
    hidden = (jax.nn.silu(summed[:, :hidden_cols]) * summed[:, hidden_cols:]).astype(jnp.bfloat16)
    ffn_part = reduce_rows(hidden, w_down).astype(jnp.bfloat16)
    return (attn_part, ffn_part)


def route_tables(ancestors, part_dev, groups):
    source_dev = (ancestors // part_dev).reshape(groups, part_dev)
    local_index = (ancestors % part_dev).reshape(groups, part_dev)
    same_source = source_dev[:, :, None] == source_dev[:, None, :]
    members = jnp.arange(part_dev, dtype=jnp.int32)
    earlier = members[None, :] < members[:, None]
    order_rank = jnp.sum((same_source & earlier[None, :, :]).astype(jnp.int32), axis=2)
    return (source_dev, local_index, order_rank)


def local(
    x_first,
    x_second,
    cache_keys,
    cache_values,
    ancestors,
    attn_gain,
    ffn_gain,
    w_query,
    w_keyval,
    w_out,
    w_gate,
    w_up,
    w_down,
):
    groups = lax.axis_size("dp")
    part_dev = x_first.shape[0]
    cache_span = cache_keys.shape[1]
    context = cache_span * lax.axis_size("tensor")
    capacity = max(2, -(-part_dev // groups))
    keys_here = cache_keys.reshape(part_dev, cache_span, KVH, HD)
    values_here = cache_values.reshape(part_dev, cache_span, KVH, HD)
    queries_one, keys_one, values_one = project_step(x_first, attn_gain, w_query, w_keyval, context)
    attn_state = merge_positions(partial_attention(queries_one, keys_here, values_here))
    mixed_one = finish(add_key(attn_state, queries_one, keys_one, values_one))
    attn_one, ffn_one = updates(x_first, mixed_one, ffn_gain, w_out, w_gate, w_up, w_down)
    queries_two, keys_two, values_two = project_step(
        x_second, attn_gain, w_query, w_keyval, context + 1
    )
    token_pairs = jnp.concatenate(
        [keys_one.reshape(part_dev, -1), values_one.reshape(part_dev, -1)], axis=1
    )
    source_dev, local_index, order_rank = route_tables(ancestors, part_dev, groups)
    device_index = lax.axis_index("dp")
    home_source = lax.dynamic_index_in_dim(source_dev, device_index, 0, keepdims=False)
    home_rank = lax.dynamic_index_in_dim(order_rank, device_index, 0, keepdims=False)
    pick_index = home_source * capacity + home_rank
    slot_ids = jnp.arange(capacity, dtype=jnp.int32)
    wanted_here = (source_dev[:, None, :] == device_index) & (
        order_rank[:, None, :] == slot_ids[None, :, None]
    )
    chosen = jnp.sum(jnp.where(wanted_here, local_index[:, None, :], 0), axis=2).reshape(-1)
    arrived = (
        lax.all_to_all(
            jnp.take(cache_keys, chosen, axis=0).reshape(groups, capacity, cache_span, -1),
            "dp",
            split_axis=0,
            concat_axis=0,
            tiled=True,
        ),
        lax.all_to_all(
            jnp.take(cache_values, chosen, axis=0).reshape(groups, capacity, cache_span, -1),
            "dp",
            split_axis=0,
            concat_axis=0,
            tiled=True,
        ),
        lax.all_to_all(
            jnp.take(token_pairs, chosen, axis=0).reshape(groups, capacity, -1),
            "dp",
            split_axis=0,
            concat_axis=0,
            tiled=True,
        ),
    )
    moved_keys = jnp.take(
        arrived[0].reshape(groups * capacity, cache_span, KVH, HD), pick_index, axis=0
    )
    moved_values = jnp.take(
        arrived[1].reshape(groups * capacity, cache_span, KVH, HD), pick_index, axis=0
    )
    moved_token = jnp.take(arrived[2].reshape(groups * capacity, -1), pick_index, axis=0)
    attn_state = partial_attention(queries_two, moved_keys, moved_values)
    attn_state = merge_positions(attn_state)
    key_width = KVH * HD
    attn_state = add_key(
        attn_state,
        queries_two,
        moved_token[:, :key_width].reshape(part_dev, KVH, HD),
        moved_token[:, key_width:].reshape(part_dev, KVH, HD),
    )
    attn_state = add_key(attn_state, queries_two, keys_two, values_two)
    mixed_two = finish(attn_state)
    attn_two, ffn_two = updates(x_second, mixed_two, ffn_gain, w_out, w_gate, w_up, w_down)
    return (jnp.stack([attn_one, attn_two]), jnp.stack([ffn_one, ffn_two]))


def solution(mesh):
    return jax.shard_map(
        local,
        mesh=mesh,
        in_specs=(
            P("dp", "tensor"),
            P("dp", "tensor"),
            P("dp", "tensor", None),
            P("dp", "tensor", None),
            P(),
            P("tensor"),
            P("tensor"),
            P("tensor", "dp"),
            P("tensor", "dp"),
            P("dp", "tensor"),
            P("tensor", "dp"),
            P("tensor", "dp"),
            P("dp", "tensor"),
        ),
        out_specs=(P(None, "dp", "tensor"), P(None, "dp", "tensor")),
        check_vma=False,
    )
```

profile of v0, /device:TPU:1, one launch (start us, length us, event | category | flops | bytes accessed | tf_op | source)
XLA Modules:
  0.0 1543.5 jit_solution(9290159140787544544)
XLA Ops:
  8.9 29.8 %all-reduce.2 = (f32[8]{0:T(128)S(1)}, f32[8]{0:T(128)S(1)}) all-reduce(f32[8]{0:T(128)S(1)} %fusion.48, f32[8]{0:T(128)S(1)} %fusion.44), channel_id=1, replica_groups=mesh['dp'=32,'tensor'=16] {'tensor'}, use_global_device_ids=true, to_apply=%region_9.0 | all-reduce | flops 16 | bytes 128 | tf_op jit(solution)/shard_map/psum | solution.py:29
  39.5 38.0 %all_gather.48 = bf16[256,512]{1,0:T(8,128)(2,1)S(1)} all-gather(bf16[8,512]{1,0:T(8,128)(2,1)S(1)} %get-tuple-element.435), channel_id=1, replica_groups=mesh['dp'=32,'tensor'=16] {'dp'}, dimensions={0}, use_global_device_ids=true | all-gather | bytes 270336 | tf_op jit(solution)/shard_map/all_gather | solution.py:37
  79.8 36.9 %all_gather.55 = bf16[256,512]{1,0:T(8,128)(2,1)S(1)} all-gather(bf16[8,512]{1,0:T(8,128)(2,1)S(1)} %get-tuple-element.436), channel_id=1, replica_groups=mesh['dp'=32,'tensor'=16] {'dp'}, dimensions={0}, use_global_device_ids=true | all-gather | bytes 270336 | tf_op jit(solution)/shard_map/all_gather | solution.py:37
  119.0 75.3 %all-reduce.8 = (bf16[256,320]{0,1:T(8,128)(2,1)S(1)}, bf16[256,320]{0,1:T(8,128)(2,1)S(1)}) all-reduce(f32[256,320]{0,1:T(8,128)S(1)} %pad_maximum_fusion.3, f32[256,320]{0,1:T(8,128)S(1)} %pad_maximum_fusion.2), channel_id=1, replica_groups=mesh['dp'=32,'tensor'=16] {'tensor'}, use_global_device_ids=true, to_apply=%region_10.0 | all-reduce | flops 163840 | bytes 983040 | tf_op jit(solution)/shard_map/psum | solution.py:71
  195.2 4.3 all-to-all-start
  200.5 8.3 all-to-all-done
  208.8 4.6 all-to-all-start.1
  221.9 7.3 all-to-all-start.7
  232.5 5.3 all-to-all-done.7
  237.9 3.9 all-to-all-start.3
  243.5 7.7 all-to-all-done.3
  251.1 3.9 all-to-all-start.6
  257.3 8.2 all-to-all-done.6
  265.6 3.9 all-to-all-start.4
  272.4 15.5 %all-to-all-done.4 = bf16[32,2,8,1024]{3,2,1,0:T(8,128)(2,1)S(1)} async-done(((bf16[32,2,8,1024]{3,2,1,0:T(8,128)(2,1)}), bf16[32,2,8,1024]{3,2,1,0:T(8,128)(2,1)S(1)}, u32[]{:S(2)}, u32[]{:S(2)}) %all-to-all-start.4) | async-done | bytes 1048608 | tf_op jit(solution)/shard_map/all_to_all | solution.py:193
  287.9 6.8 all-to-all-start.5
  295.7 29.2 %all-gather = f32[128,8,8]{2,1,0:T(8,128)S(1)} all-gather(f32[8,8,8]{2,1,0:T(8,128)S(1)} %copy-done.10), channel_id=2, replica_groups=mesh['dp'=32,'tensor'=16] {'tensor'}, dimensions={0}, use_global_device_ids=true | all-gather | bytes 34816 | tf_op jit(solution)/shard_map/all_gather | solution.py:18
  325.0 16.1 %all-gather.1 = f32[128,8,8]{2,1,0:T(8,128)S(1)} all-gather(f32[8,8,8]{2,1,0:T(8,128)S(1)} %fusion.9), channel_id=3, replica_groups=mesh['dp'=32,'tensor'=16] {'tensor'}, dimensions={0}, use_global_device_ids=true | all-gather | bytes 34816 | tf_op jit(solution)/shard_map/all_gather | solution.py:18
  352.9 19.2 %while.38 = (s32[]{:T(128)}, f32[8,8,8]{2,1,0:T(8,128)S(1)}, f32[8,8,8]{2,1,0:T(8,128)S(1)}, f32[8,8,8,128]{3,2,1,0:T(8,128)S(1)}, f32[16,8,8,8]{3,2,1,0:T(8,128...) while((s32[]{:T(128)}, f32[8,8,8]{2,1,0:T(8,128)S(1)}, ...), condition=%wide.region_6.0_spmd, body=%wide.region_5.0_spmd.sunk | while | flops 199685 | bytes 807055 | solution.py:24
  373.2 9.5 all-to-all-start.2
  383.0 17.9 %all-gather.3 = f32[128,8,8]{2,1,0:T(8,128)S(1)} all-gather(f32[8,8,8]{2,1,0:T(8,128)S(1)} %get-tuple-element.441), channel_id=5, replica_groups=mesh['dp'=32,'tensor'=16] {'tensor'}, dimensions={0}, use_global_device_ids=true | all-gather | bytes 34816 | tf_op jit(solution)/shard_map/all_gather | solution.py:18
  401.0 16.2 %all-gather.4 = f32[128,8,8]{2,1,0:T(8,128)S(1)} all-gather(f32[8,8,8]{2,1,0:T(8,128)S(1)} %fusion.11), channel_id=6, replica_groups=mesh['dp'=32,'tensor'=16] {'tensor'}, dimensions={0}, use_global_device_ids=true | all-gather | bytes 34816 | tf_op jit(solution)/shard_map/all_gather | solution.py:18
  419.3 19.2 %while.39 = (s32[]{:T(128)}, f32[8,8,8]{2,1,0:T(8,128)S(1)}, f32[8,8,8]{2,1,0:T(8,128)S(1)}, f32[8,8,8,128]{3,2,1,0:T(8,128)S(1)}, f32[16,8,8,8]{3,2,1,0:T(8,128...) while((s32[]{:T(128)}, f32[8,8,8]{2,1,0:T(8,128)S(1)}, ...), condition=%wide.region_16.19_spmd, body=%wide.region_15.18_spmd.sunk | while | flops 199685 | bytes 807055 | solution.py:24
  439.2 19.2 %all_to_all.105 = bf16[8,32,256]{2,0,1:T(8,128)(2,1)S(1)} all-to-all(bf16[8,32,256]{2,0,1:T(8,128)(2,1)S(1)} %copy.99), channel_id=1, replica_groups=mesh['dp'=32,'tensor'=16] {'dp'}, dimensions={1} | all-to-all | bytes 262144 | tf_op jit(solution)/shard_map/all_to_all | solution.py:126
  459.3 170.9 %reduce-scatter.5.cloned.1.call-done = bf16[8,512]{1,0:T(8,128)(2,1)} async-done(((bf16[256,512]{1,0:T(8,128)(2,1)}), bf16[8,512]{1,0:T(8,128)(2,1)}) %reduce-scatter.5.cloned.1.call-update) | async-done | bytes 8208 | tf_op jit(solution)/shard_map/reduce_scatter | solution.py:44
  631.1 220.8 %reduce-scatter.7.cloned.1.call-done = bf16[8,512]{1,0:T(8,128)(2,1)} async-done(((bf16[256,512]{1,0:T(8,128)(2,1)}), bf16[8,512]{1,0:T(8,128)(2,1)}) %reduce-scatter.7.cloned.1.call-update) | async-done | bytes 8208 | tf_op jit(solution)/shard_map/reduce_scatter | solution.py:44
  852.7 28.8 %all-reduce = (f32[8]{0:T(128)S(1)}, f32[8]{0:T(128)S(1)}) all-reduce(f32[8]{0:T(128)S(1)} %fusion.41, f32[8]{0:T(128)S(1)} %fusion.38), channel_id=1, replica_groups=mesh['dp'=32,'tensor'=16] {'tensor'}, use_global_device_ids=true, to_apply=%region_23.26 | all-reduce | flops 16 | bytes 128 | tf_op jit(solution)/shard_map/psum | solution.py:29
  882.3 35.6 %all_gather.62 = bf16[256,512]{1,0:T(8,128)(2,1)S(1)} all-gather(bf16[8,512]{1,0:T(8,128)(2,1)S(1)} %get-tuple-element.433), channel_id=1, replica_groups=mesh['dp'=32,'tensor'=16] {'dp'}, dimensions={0}, use_global_device_ids=true | all-gather | bytes 270336 | tf_op jit(solution)/shard_map/all_gather | solution.py:37
  918.5 35.0 %all_gather.63 = bf16[256,512]{1,0:T(8,128)(2,1)S(1)} all-gather(bf16[8,512]{1,0:T(8,128)(2,1)S(1)} %get-tuple-element.434), channel_id=1, replica_groups=mesh['dp'=32,'tensor'=16] {'dp'}, dimensions={0}, use_global_device_ids=true | all-gather | bytes 270336 | tf_op jit(solution)/shard_map/all_gather | solution.py:37
  955.9 138.6 %all-reduce.7.cloned.1.call-done = (bf16[256,896]{0,1:T(8,128)(2,1)}, bf16[256,896]{0,1:T(8,128)(2,1)}) async-done(((bf16[256,896]{0,1:T(8,128)(2,1)}, bf16[256,896]{0,1:T(8,128)(2,1)}), (bf16[256,896]{0,1:T(8,128)(2,1)}, bf16[256,896]{0,1:T(8,128)(2,1)})) %all-reduce.7.cloned.1.call-update) | async-done | bytes 917520 | tf_op jit(solution)/shard_map/psum | solution.py:134
  1098.6 215.4 %reduce-scatter.11.cloned.1.call-done = bf16[8,512]{1,0:T(8,128)(2,1)} async-done(((bf16[256,512]{1,0:T(8,128)(2,1)}), bf16[8,512]{1,0:T(8,128)(2,1)}) %reduce-scatter.11.cloned.1.call-update) | async-done | bytes 8208 | tf_op jit(solution)/shard_map/reduce_scatter | solution.py:44
  1314.1 221.3 %reduce-scatter.9.cloned.1.call-done = bf16[8,512]{1,0:T(8,128)(2,1)} async-done(((bf16[256,512]{1,0:T(8,128)(2,1)}), bf16[8,512]{1,0:T(8,128)(2,1)}) %reduce-scatter.9.cloned.1.call-update) | async-done | bytes 8208 | tf_op jit(solution)/shard_map/reduce_scatter | solution.py:44
  (274 shorter events, 93.5 us)
Async XLA Ops:
  7.2 1088.4 %copy-start = (bf16[448,512]{1,0:T(8,128)(2,1)S(1)}, bf16[448,512]{1,0:T(8,128)(2,1)}, u32[]{:S(2)}) copy-start(bf16[448,512]{1,0:T(8,128)(2,1)} %param.33) | copy-start | bytes 1376260
  7.2 192.3 %copy-start.32 = (s32[256]{0:T(256)S(1)}, s32[256]{0:T(256)}, u32[]{:S(2)}) copy-start(s32[256]{0:T(256)} %param.25) | copy-start | bytes 3076
  7.2 206.5 %copy-start.2 = (bf16[8,8,1024]{2,1,0:T(8,128)(2,1)S(1)}, bf16[8,8,1024]{2,1,0:T(8,128)(2,1)}, u32[]{:S(2)}) copy-start(bf16[8,8,1024]{2,1,0:T(8,128)(2,1)} %param.23) | copy-start | bytes 393220
  78.5 135.5 %copy-start.1 = (bf16[8,8,1024]{2,1,0:T(8,128)(2,1)S(1)}, bf16[8,8,1024]{2,1,0:T(8,128)(2,1)}, u32[]{:S(2)}) copy-start(bf16[8,8,1024]{2,1,0:T(8,128)(2,1)} %param.24) | copy-start | bytes 393220
  195.2 13.6 all-to-all-start
  208.8 13.2 all-to-all-start.1
  213.3 138.5 %all-gather.9.cloned.1.call-start = ((), (), s32[]{:S(2)}) async-start(), calls=%async_computation.17 | async-start | bytes 4456448 | tf_op jit(solution)/shard_map/all_gather | solution.py:18
  221.9 15.9 %all-to-all-start.7 = ((bf16[32,2,256]{2,1,0:T(2,128)(2,1)}), bf16[32,2,256]{2,1,0:T(2,128)(2,1)S(1)}, u32[]{:S(2)}, u32[]{:S(2)}) async-start(bf16[32,2,256]{2,1,0:T(2,128)(2,1)} %reshape.390), calls=%async_computation.8 | async-start | bytes 65536 | tf_op jit(solution)/shard_map/all_to_all | solution.py:75
  232.3 37.2 %copy-start.21 = (s32[32,8]{0,1:T(8,128)S(1)}, s32[32,8]{0,1:T(8,128)}, u32[]{:S(2)}) copy-start(s32[32,8]{0,1:T(8,128)} %copy-done.20) | copy-start | bytes 3076
  232.3 37.2 %copy-start.23 = (s32[32,8]{0,1:T(8,128)S(1)}, s32[32,8]{0,1:T(8,128)}, u32[]{:S(2)}) copy-start(s32[32,8]{0,1:T(8,128)} %copy-done.22) | copy-start | bytes 3076
  237.9 13.2 all-to-all-start.3
  251.1 14.4 all-to-all-start.6
  257.3 37.5 %copy-start.13 = (bf16[8,8,64]{2,1,0:T(8,128)(2,1)S(1)}, bf16[8,8,64]{2,1,0:T(8,128)(2,1)}, u32[]{:S(2)}) copy-start(bf16[8,8,64]{2,1,0:T(8,128)(2,1)} %copy-done.12) | copy-start | bytes 24580
  257.3 38.4 %copy-start.10 = (f32[8,8,8]{2,1,0:T(8,128)S(1)}, f32[8,8,8]{2,1,0:T(8,128)}, u32[]{:S(2)}) copy-start(f32[8,8,8]{2,1,0:T(8,128)} %copy-done.9) | copy-start | bytes 6148
  265.6 22.3 %all-to-all-start.4 = ((bf16[32,2,8,1024]{3,2,1,0:T(8,128)(2,1)}), bf16[32,2,8,1024]{3,2,1,0:T(8,128)(2,1)S(1)}, u32[]{:S(2)}, u32[]{:S(2)}) async-start(bf16[32,2,8,1024]{3,2,1,0:T(8,128)(2,1)} %bitcast.159), calls=%async_computation.5 | async-start | bytes 2097152 | tf_op jit(solution)/shard_map/all_to_all | solution.py:193
  269.8 55.1 %copy-start.29 = (f32[64]{0:T(128)}, f32[64]{0:T(128)S(1)}, u32[]{:S(2)}) copy-start(f32[64]{0:T(128)S(1)} %get-tuple-element.447) | copy-start | bytes 772
  269.8 55.1 %copy-start.30 = (f32[64]{0:T(128)}, f32[64]{0:T(128)S(1)}, u32[]{:S(2)}) copy-start(f32[64]{0:T(128)S(1)} %get-tuple-element.448) | copy-start | bytes 772
  287.9 59.0 %all-to-all-start.5 = ((bf16[32,2,8,1024]{3,2,1,0:T(8,128)(2,1)}), bf16[32,2,8,1024]{3,2,1,0:T(8,128)(2,1)}, u32[]{:S(2)}, u32[]{:S(2)}) async-start(bf16[32,2,8,1024]{3,2,1,0:T(8,128)(2,1)} %bitcast.158), calls=%async_computation.6 | async-start | bytes 2097152 | tf_op jit(solution)/shard_map/all_to_all | solution.py:200
  294.6 123.7 %all-gather.11.cloned.1.call-start = ((), (), s32[]{:S(2)}) async-start(), calls=%async_computation.18 | async-start | bytes 4456448 | tf_op jit(solution)/shard_map/all_gather | solution.py:18
  352.9 64.4 %copy-start.5 = (bf16[256,512]{1,0:T(8,128)(2,1)S(1)}, bf16[256,512]{1,0:T(8,128)(2,1)}, u32[]{:S(2)}) copy-start(bf16[256,512]{1,0:T(8,128)(2,1)} %param.30) | copy-start | bytes 786436
  373.2 44.1 %all-to-all-start.2 = ((bf16[8,32,256]{2,0,1:T(8,128)(2,1)}), bf16[8,32,256]{2,0,1:T(8,128)(2,1)S(1)}, u32[]{:S(2)}, u32[]{:S(2)}) async-start(bf16[8,32,256]{2,0,1:T(8,128)(2,1)} %copy.84), calls=%async_computation.2 | async-start | bytes 262144 | tf_op jit(solution)/shard_map/all_to_all | solution.py:126
  382.6 247.7 %reduce-scatter.5.cloned.1.call-start = ((), (), s32[]{:S(2)}) async-start(), calls=%async_computation.13 | async-start | bytes 270336 | tf_op jit(solution)/shard_map/reduce_scatter | solution.py:44
  400.9 37.7 %copy-start.14 = (f32[8,8,128]{2,1,0:T(8,128)S(1)}, f32[8,8,128]{2,1,0:T(8,128)}, u32[]{:S(2)}) copy-start(f32[8,8,128]{2,1,0:T(8,128)} %get-tuple-element.431) | copy-start | bytes 98308
  418.2 433.7 %reduce-scatter.7.cloned.1.call-start = ((), (), s32[]{:S(2)}) async-start(), calls=%async_computation.14 | async-start | bytes 270336 | tf_op jit(solution)/shard_map/reduce_scatter | solution.py:44
  419.3 211.0 %copy-start.16 = (bf16[8,512]{1,0:T(8,128)(2,1)S(1)}, bf16[8,512]{1,0:T(8,128)(2,1)}, u32[]{:S(2)}) copy-start(bf16[8,512]{1,0:T(8,128)(2,1)} %param.21) | copy-start | bytes 24580
  419.3 432.6 %copy-start.17 = (bf16[8,512]{1,0:T(8,128)(2,1)S(1)}, bf16[8,512]{1,0:T(8,128)(2,1)}, u32[]{:S(2)}) copy-start(bf16[8,512]{1,0:T(8,128)(2,1)} %param.22) | copy-start | bytes 24580
  419.3 462.2 %copy-start.31 = (f32[512]{0:T(512)S(1)}, f32[512]{0:T(512)}, u32[]{:S(2)}) copy-start(f32[512]{0:T(512)} %param.27) | copy-start | bytes 6148
  419.3 498.6 %copy-start.3 = (bf16[512,448]{0,1:T(8,128)(2,1)S(1)}, bf16[512,448]{0,1:T(8,128)(2,1)}, u32[]{:S(2)}) copy-start(bf16[512,448]{0,1:T(8,128)(2,1)} %param.32) | copy-start | bytes 1376260
  419.3 498.9 %copy-start.4 = (bf16[512,448]{0,1:T(8,128)(2,1)S(1)}, bf16[512,448]{0,1:T(8,128)(2,1)}, u32[]{:S(2)}) copy-start(bf16[512,448]{0,1:T(8,128)(2,1)} %param.31) | copy-start | bytes 1376260
  459.3 635.2 %all-reduce.7.cloned.1.call-start = ((), (), s32[]{:S(2)}) async-start(), calls=%async_computation.19 | async-start | bytes 1835008 | tf_op jit(solution)/shard_map/psum | solution.py:134
  955.9 358.2 %reduce-scatter.11.cloned.1.call-start = ((), (), s32[]{:S(2)}) async-start(), calls=%async_computation.16 | async-start | bytes 270336 | tf_op jit(solution)/shard_map/reduce_scatter | solution.py:44
  1096.7 438.6 %reduce-scatter.9.cloned.1.call-start = ((), (), s32[]{:S(2)}) async-start(), calls=%async_computation.15 | async-start | bytes 270336 | tf_op jit(solution)/shard_map/reduce_scatter | solution.py:44
  (17 other events, 155.2 us)
Sparse Core Ops, SparseCore 0:
  216.3 48.0 all-gather.8
  351.9 43.4 all-gather.10
  418.3 211.9 reduce-scatter.4
  635.2 216.6 reduce-scatter.6
  956.0 138.4 all-reduce.6
  1099.3 214.6 reduce-scatter.10
  1318.4 216.8 reduce-scatter.8
where the time goes:
time: 1550 us; the launch traced here: 1540 us
  waiting for transfers between devices  1010 us (65%)
  blocking collectives  378 us (24%)
  other arithmetic  58.3 us (4%)
  starting transfers between devices  44.3 us (3%)
  matrix products  16.7 us (1%)
  local copies, waits for them, and re-layouts  16.2 us (1%)
    reduce_scatter x4, waiting for transfers between devices, reduce_rows(): lax.psum_scatter(jnp.dot(left, weight, preferred_element_type=jnp.float32...  828 us
    all_gather x4, blocking collectives, project_rows(): piece = lax.all_gather(normed, 'dp', axis=0, tiled=True)  146 us
    psum x1, waiting for transfers between devices, updates(): lax.psum(partial_value.astype(jnp.bfloat16), 'tensor').astype(jnp.float32)  139 us
    all_gather x4, blocking collectives, combined_all(): everything = jax.tree.map(lambda part: lax.all_gather(part, axis), x)  79.4 us
    psum x1, blocking collectives, project_step(): summed = lax.psum(partial_value, 'tensor').astype(jnp.bfloat16)  75.3 us
    psum x2, blocking collectives, normalize(): squares = lax.psum(jnp.sum(wide * wide, axis=1), 'tensor')  58.5 us
    add x30, other arithmetic, combine(): first[2] * first_scale[..., None] + second[2] * second_scale[..., None]  36.5 us
  transfers between devices with their start and end apart: 15, of which 11 were waited for; matrix products, arithmetic and copies ran while one was open for 5% of the time, Pallas kernels for 0%

commit v1 on v0

v1 whole, which is shorter than its diff:
```python
import math

import jax
import jax.numpy as jnp
from jax import lax
from jax.sharding import Mesh, PartitionSpec as P

NZ, NX, NY, NC = 8, 4, 8, 2
HD = 128
GROUP = 8
EPS = 1e-05
ROPE_BASE = 500000.0
DP = ("z", "x")
TENSOR = ("y", "c")
F32 = jnp.float32
BF16 = jnp.bfloat16
LOW = -1e30


def exchange(blocks, axes):
    return lax.all_to_all(blocks, axes, split_axis=0, concat_axis=0, tiled=True)


def spread(block, axes, count):
    return exchange(jnp.broadcast_to(block[None], (count, *block.shape)), axes)


def dot(a, b):
    return jnp.dot(a, b, preferred_element_type=F32)


def split_hi_lo(value):
    hi = value.astype(BF16)
    return hi, (value - hi.astype(F32)).astype(BF16)


def tables(ancestors, block, half):
    anc = ancestors.reshape(NZ * NX, 8)
    earlier = jnp.tril(jnp.ones((8, 8), jnp.int32), -1)
    mine = lax.dynamic_index_in_dim(anc, block, 0, keepdims=False)
    mine_block, mine_half = mine // 8, (mine // 4) % 2
    quad = mine // 4
    rank = jnp.sum((quad[:, None] == quad[None, :]) * earlier, axis=1)
    i = jnp.arange(NZ * NX)[:, None, None, None]
    head = jnp.arange(8)[None, :, None, None]
    slot = jnp.arange(2)[None, None, :, None]
    col = jnp.arange(128)[None, None, None, :]
    particle = (col // 8) % 2 * 4 + col % 4
    col_block, col_half, col_rank = (
        jnp.broadcast_to(v.reshape(1, 2, 1, 4), (8, 2, 2, 4)).reshape(1, 1, 1, 128)
        for v in (mine_block, mine_half, rank)
    )
    hit = (
        (col // 16 == head)
        & ((col // 4) % 2 == 1)
        & (col_block == i)
        & (col_half == half)
        & (col_rank == slot)
        & (particle >= 0)
    )
    select = hit.astype(BF16).reshape(512, 128)
    wanted = anc // 4 == block * 2 + half
    order = jnp.sum(wanted[:, None, :] * earlier[None], axis=2)
    which = jnp.stack(
        [jnp.sum(jnp.where(wanted & (order == s), anc % 4, 0), axis=1) for s in range(2)], axis=1
    )
    which = jnp.broadcast_to(which[:, None, :], (NZ * NX, 8, 2)).reshape(512, 1)
    own = jnp.broadcast_to(jnp.arange(128)[:, None] % 4, (128, 1))
    return select, jnp.concatenate([which, own], axis=0).astype(jnp.int32)


def angles(position):
    freq = jnp.power(F32(ROPE_BASE), -2.0 * jnp.arange(HD // 2, dtype=F32) / HD)
    angle = F32(position) * freq
    return jnp.cos(angle), jnp.sin(angle)


def rotate(rows, context):
    tables_ = [angles(context), angles(context + 1)]
    cos = jnp.stack([jnp.concatenate([c, c]) for c, _ in tables_])
    sin = jnp.stack([jnp.concatenate([-s, s]) for _, s in tables_])
    step = (jnp.arange(rows.shape[0]) // 4) % 2
    cos = jnp.where(step[:, None] == 0, cos[0], cos[1])
    sin = jnp.where(step[:, None] == 0, sin[0], sin[1])
    turned = jnp.concatenate([rows[:, 64:], rows[:, :64]], axis=1)
    return rows * cos + turned * sin


def attend(queries, keys, values, which, own_key, own_value, half):
    scale = 1.0 / math.sqrt(HD)
    scores = lax.dot_general(
        queries, keys, (((1,), (1,)), ((), ())), preferred_element_type=F32
    ) * scale
    k = jnp.arange(640)[None, :]
    new = k - 512
    key_particle = jnp.where(k < 512, (k // 8) % 4, k % 4)
    key_ok = (k < 512) | ((new < 16) & ((new // 4) % 2 == 0) & (new // 8 == half))
    scores = jnp.where((key_particle == which) & key_ok, scores, LOW)
    own = jnp.sum(queries[:512].astype(F32) * own_key, axis=1, keepdims=True) * scale
    own = jnp.concatenate([own, jnp.full((128, 1), LOW, F32)], axis=0)
    highest = jnp.maximum(jnp.max(scores, axis=1, keepdims=True), own)
    weights = jnp.exp(scores - highest)
    own = jnp.exp(own - highest)
    totals = jnp.sum(weights, axis=1, keepdims=True) + own
    mixed = dot(weights.astype(BF16), values)
    extra = jnp.concatenate([own[:512] * own_value, jnp.zeros((128, HD), F32)], axis=0)
    return ((mixed + extra) / totals).astype(BF16)


def sum_blocks(blocks):
    return jnp.sum(blocks.astype(F32), axis=0)


def local(
    x_first, x_second, cache_keys, cache_values, ancestors, attn_gain, ffn_gain,
    w_query, w_keyval, w_out, w_gate, w_up, w_down,
):
    z, x, y, c = (lax.axis_index(a) for a in ("z", "x", "y", "c"))
    context = cache_keys.shape[1] * NY * NC
    width = x_first.shape[1] * NY * NC
    dp, ff = NZ * NX, w_gate.shape[1]
    select, which = tables(ancestors, y * NX + x, c)

    cache = jnp.stack([cache_keys, cache_values]).reshape(2, 8, 8, 8, HD)
    cache = exchange(cache.transpose(3, 0, 1, 2, 4), ("z",))
    cache = cache.reshape(8, 2, 2, 4, 8, HD).transpose(0, 2, 1, 3, 4, 5).reshape(16, 2, 32, HD)
    cache = exchange(cache, TENSOR).transpose(1, 0, 2, 3).reshape(2, 512, HD)

    moves = [(s, (s % 16) // 2 * NX + s // 16 * 2 + s % 2) for s in range(dp)]
    w_keyval = lax.ppermute(w_keyval, DP, moves)

    rows = jnp.stack([x_first.reshape(2, 4, -1), x_second.reshape(2, 4, -1)], axis=1).reshape(16, -1)
    wide = spread(rows, DP, dp).reshape(512, -1).astype(F32)
    squares = jnp.concatenate(split_hi_lo(jnp.sum(wide * wide, axis=1, keepdims=True)), axis=1)
    scaled = (wide * attn_gain[None, :]).astype(BF16)
    part = dot(scaled, jnp.concatenate([w_query, w_keyval], axis=1)).astype(BF16)
    part = jnp.concatenate([part, jnp.pad(squares, ((0, 0), (0, 62)))], axis=1)
    part = part.reshape(NZ, NX, 2, 8, 384).transpose(0, 2, 1, 3, 4).reshape(16, 32, 384)
    total = sum_blocks(exchange(part, TENSOR))
    factor = lax.rsqrt((total[:, 320:321] + total[:, 321:322]) / width + EPS)
    heads = (total[:, :320] * factor).astype(BF16).reshape(NX, 1, 8, 320)
    heads = exchange(jnp.broadcast_to(heads, (NX, NC, 8, 320)).reshape(8, 8, 320), ("x", "c"))
    heads = heads.reshape(NX, 16, 320).astype(F32)

    queries = heads[:, :, :256].reshape(NX, 16, 2, HD).transpose(0, 2, 1, 3).reshape(128, HD)
    queries = rotate(queries, context).astype(BF16)
    new_keys = rotate(jnp.concatenate([heads[0, :, 256:], heads[1, :, 256:]], axis=1), context)
    new_keys = new_keys.astype(BF16)
    new_values = jnp.concatenate([heads[2, :, 256:], heads[3, :, 256:]], axis=1).astype(BF16)

    pairs = jnp.concatenate([new_keys, new_values, jnp.zeros((96, HD), BF16)], axis=0)
    send = jnp.concatenate([dot(select, queries), dot(select, pairs_for(pairs))], axis=1)
    got = exchange(send.astype(BF16).reshape(dp, 16, 256), ("y", "x")).reshape(512, 256)
    row = jnp.arange(512)[:, None]
    col = jnp.arange(512)[None, :]
    same = (row // 16 == col // 16) & (row % 2 == col % 2)
    own_key = dot((same & (col // 2 % 8 == 0)).astype(BF16), got[:, HD:])
    own_value = dot((same & (col // 2 % 8 == 1)).astype(BF16), got[:, HD:])
    pad = jnp.zeros((112, HD), BF16)
    mixed = attend(
        jnp.concatenate([got[:, :HD], queries], axis=0),
        jnp.concatenate([cache[0], new_keys, pad], axis=0),
        jnp.concatenate([cache[1], new_values, pad], axis=0),
        which, own_key, own_value, c,
    )
    back = exchange(mixed[:512].reshape(dp, 16, HD), ("y", "x")).reshape(512, HD)
    second = lax.dot_general(select, back, (((0,), (0,)), ((), ())), preferred_element_type=F32)
    r = jnp.arange(128)[:, None]
    first = jnp.where(((r // 4) % 2 == 0) & ((r // 8) % 2 == c), mixed[512:].astype(F32), 0.0)
    mixed = (first + second).astype(BF16).reshape(NX, 2, 16, HD).transpose(0, 2, 1, 3)
    mixed = mixed.reshape(NX, 1, 16, 256)
    mixed = exchange(jnp.broadcast_to(mixed, (NX, NC, 16, 256)).reshape(8, 16, 256), ("x", "c"))
    mixed = jnp.sum(mixed.reshape(NX, NC, 16, 256), axis=1).reshape(64, 256)
    mixed = spread(mixed, ("y",), NY).reshape(512, 256)

    part = dot(mixed, w_out).astype(BF16).reshape(dp, 16, -1)
    attn = sum_blocks(exchange(part, DP)).astype(BF16)
    residual = (rows.astype(F32) + attn.astype(F32)).astype(BF16)

    wide = spread(residual, DP, dp).reshape(512, -1).astype(F32)
    squares = jnp.concatenate(split_hi_lo(jnp.sum(wide * wide, axis=1, keepdims=True)), axis=1)
    scaled = (wide * ffn_gain[None, :]).astype(BF16)
    gate = jnp.concatenate(
        [dot(scaled, w_gate).astype(BF16), jnp.pad(squares, ((0, 0), (0, 62)))], axis=1
    )
    up = jnp.pad(dot(scaled, w_up).astype(BF16), ((0, 0), (0, 64)))
    part = jnp.concatenate([gate, up], axis=1).reshape(16, 32, 2 * (ff + 64))
    total = sum_blocks(exchange(part, TENSOR))
    factor = lax.rsqrt((total[:, ff : ff + 1] + total[:, ff + 1 : ff + 2]) / width + EPS)
    gate, up = total[:, :ff] * factor, total[:, ff + 64 : 2 * ff + 64] * factor
    hidden = (gate / (1.0 + jnp.exp(-gate)) * up).astype(BF16)
    hidden = spread(hidden, TENSOR, NY * NC).reshape(512, ff)
    part = dot(hidden, w_down).astype(BF16).reshape(dp, 16, -1)
    ffn = sum_blocks(exchange(part, DP)).astype(BF16)

    def by_step(block):
        return block.reshape(2, 2, 4, -1).transpose(1, 0, 2, 3).reshape(2, 8, -1)

    return by_step(attn), by_step(ffn)


def pairs_for(pairs):
    return jnp.concatenate([pairs[:32], jnp.zeros((96, HD), BF16)], axis=0)


def solution(mesh):
    fine = Mesh(mesh.devices.reshape(NZ, NX, NY, NC), ("z", "x", "y", "c"))
    rows, cols = P(TENSOR, DP), P(DP, TENSOR)
    return jax.shard_map(
        local,
        mesh=fine,
        in_specs=(
            cols, cols, P(DP, TENSOR, None), P(DP, TENSOR, None), P(), P(TENSOR), P(TENSOR),
            rows, rows, cols, rows, rows, cols,
        ),
        out_specs=(P(None, DP, TENSOR), P(None, DP, TENSOR)),
        check_vma=False,
    )
```

time: 1550 us -> 281 us (0.18)
  waiting for transfers between devices: 1010 us -> 90.5 us
  blocking collectives: 378 us -> 117 us
  other arithmetic: 58.3 us -> 4.19 us
    reduce_scatter x4 -> x0, waiting for transfers between devices: 828 us -> none  [reduce_rows(): lax.psum_scatter(jnp.dot(left, weight, preferred_element_type=jnp.float32...]
    all_gather x8 -> x0, blocking collectives: 225 us -> none  [the longest x4 146 us: project_rows(): piece = lax.all_gather(normed, 'dp', axis=0, tiled=True)]
    psum x1 -> x0, waiting for transfers between devices: 139 us -> none  [updates(): lax.psum(partial_value.astype(jnp.bfloat16), 'tensor').astype(jnp.float32)]
    psum x3 -> x0, blocking collectives: 134 us -> none  [the longest x1 75.3 us: project_step(): summed = lax.psum(partial_value, 'tensor').astype(jnp.bfloat16)]
    all_to_all x1 -> x6, blocking collectives: 19.2 us -> 117 us  [exchange(): return lax.all_to_all(blocks, axes, split_axis=0, concat_axis=0, tiled=True)]
    all_to_all x8, waiting for transfers between devices: 46.9 us -> 90.5 us  [exchange(): return lax.all_to_all(blocks, axes, split_axis=0, concat_axis=0, tiled=True)]
    add x63 -> x1, other arithmetic: 37.7 us -> 0.02 us  [attend(): totals = jnp.sum(weights, axis=1, keepdims=True) + own]
  transfers between devices with their start and end apart: 15 -> 9, of which waited for: 11 -> 8; matrix products, arithmetic and copies ran while one was open for 5% -> 2% of each run, Pallas kernels for 0% -> 0%
where the time goes in v1:
time: 281 us; the launch traced here: 280 us
  blocking collectives  117 us (42%)
  waiting for transfers between devices  90.5 us (32%)
  starting transfers between devices  50.6 us (18%)
  local copies, waits for them, and re-layouts  10.5 us (4%)
  matrix products  5.58 us (2%)
  other arithmetic  4.19 us (1%)
    all_to_all x6, blocking collectives, exchange(): return lax.all_to_all(blocks, axes, split_axis=0, concat_axis=0, tiled=True)  117 us
    all_to_all x8, waiting for transfers between devices, exchange(): return lax.all_to_all(blocks, axes, split_axis=0, concat_axis=0, tiled=True)  90.5 us
    all_to_all x8, starting transfers between devices, exchange(): return lax.all_to_all(blocks, axes, split_axis=0, concat_axis=0, tiled=True)  49.9 us
  transfers between devices with their start and end apart: 9, of which 8 were waited for; matrix products, arithmetic and copies ran while one was open for 2% of the time, Pallas kernels for 0%

profile of v1, /device:TPU:1, one launch (start us, length us, event | category | flops | bytes accessed | tf_op | source)
XLA Modules:
  0.0 279.7 jit_solution(8352458956143049606)
XLA Ops:
  0.7 0.8 stack_reshape.7
  1.5 0.7 stack_reshape.6
  2.2 0.8 broadcast_in_dim.200
  3.1 13.8 %all-to-all-start = ((bf16[32,16,512]{2,1,0:T(8,128)(2,1)}), bf16[32,16,512]{2,1,0:T(8,128)(2,1)S(1)}, u32[]{:S(2)}, u32[]{:S(2)}) async-start(bf16[32,16,512]{2,1,0:T(8,128)(2,1)} %broadcast_in_dim.200), calls=%async_computation | async-start | bytes 1048576 | tf_op jit(solution)/shard_map/all_to_all | solution.py:21
  16.9 0.7 collective-permute-start
  19.2 0.8 copy.132
  20.2 12.9 %all-to-all-done = bf16[32,16,512]{2,1,0:T(8,128)(2,1)S(1)} async-done(((bf16[32,16,512]{2,1,0:T(8,128)(2,1)}), bf16[32,16,512]{2,1,0:T(8,128)(2,1)S(1)}, u32[]{:S(2)}, u32[]{:S(2)}) %all-to-all-start) | async-done | bytes 524320 | tf_op jit(solution)/shard_map/all_to_all | solution.py:21
  34.2 0.8 copy.122
  35.0 10.1 %all-to-all-start.1 = ((bf16[16,32,384]{2,1,0:T(8,128)(2,1)}), bf16[16,32,384]{2,1,0:T(8,128)(2,1)S(1)}, u32[]{:S(2)}, u32[]{:S(2)}) async-start(bf16[16,32,384]{2,1,0:T(8,128)(2,1)} %bitcast.10), calls=%async_computation.1 | async-start | bytes 786432 | tf_op jit(solution)/shard_map/all_to_all | solution.py:21
  45.2 14.4 %all-to-all-done.1 = bf16[16,32,384]{2,1,0:T(8,128)(2,1)S(1)} async-done(((bf16[16,32,384]{2,1,0:T(8,128)(2,1)}), bf16[16,32,384]{2,1,0:T(8,128)(2,1)S(1)}, u32[]{:S(2)}, u32[]{:S(2)}) %all-to-all-start.1) | async-done | bytes 393248 | tf_op jit(solution)/shard_map/all_to_all | solution.py:21
  59.6 5.8 %all-to-all-start.4 = ((bf16[8,2,8,8,128]{4,3,2,1,0:T(8,128)(2,1)}), bf16[8,2,8,8,128]{4,3,2,1,0:T(8,128)(2,1)S(1)}, u32[]{:S(2)}, u32[]{:S(2)}) async-start(bf16[8,2,8,8,128]{4,3,2,1,0:T(8,128)(2,1)} %copy.132), calls=%async_computation.4 | async-start | bytes 524288 | tf_op jit(solution)/shard_map/all_to_all | solution.py:21
  65.7 12.1 %all-to-all-done.4 = bf16[8,2,8,8,128]{4,3,2,1,0:T(8,128)(2,1)S(1)} async-done(((bf16[8,2,8,8,128]{4,3,2,1,0:T(8,128)(2,1)}), bf16[8,2,8,8,128]{4,3,2,1,0:T(8,128)(2,1)S(1)}, u32[]{:S(2)}, u32[]{:S(2)}) %all-to-all-start.4) | async-done | bytes 262176 | tf_op jit(solution)/shard_map/all_to_all | solution.py:21
  78.4 3.6 %all-to-all-start.2 = ((bf16[8,8,320]{2,1,0:T(8,128)(2,1)}), bf16[8,8,320]{2,1,0:T(8,128)(2,1)S(1)}, u32[]{:S(2)}, u32[]{:S(2)}) async-start(bf16[8,8,320]{2,1,0:T(8,128)(2,1)} %bitcast.12), calls=%async_computation.2 | async-start | bytes 98304 | tf_op jit(solution)/shard_map/all_to_all | solution.py:21
  82.3 0.7 copy.133
  83.1 3.8 %all-to-all-done.2 = bf16[8,8,320]{2,1,0:T(8,128)(2,1)S(1)} async-done(((bf16[8,8,320]{2,1,0:T(8,128)(2,1)}), bf16[8,8,320]{2,1,0:T(8,128)(2,1)S(1)}, u32[]{:S(2)}, u32[]{:S(2)}) %all-to-all-start.2) | async-done | bytes 40992 | tf_op jit(solution)/shard_map/all_to_all | solution.py:21
  86.9 4.1 %all-to-all-start.5 = ((bf16[16,2,32,128]{3,2,1,0:T(8,128)(2,1)}), bf16[16,2,32,128]{3,2,1,0:T(8,128)(2,1)S(1)}, u32[]{:S(2)}, u32[]{:S(2)}) async-start(bf16[16,2,32,128]{3,2,1,0:T(8,128)(2,1)} %bitcast.31), calls=%async_computation.5 | async-start | bytes 524288 | tf_op jit(solution)/shard_map/all_to_all | solution.py:21
  92.0 0.7 pad_maximum_fusion.1
  92.7 10.1 %all-to-all-done.5 = bf16[16,2,32,128]{3,2,1,0:T(8,128)(2,1)S(1)} async-done(((bf16[16,2,32,128]{3,2,1,0:T(8,128)(2,1)}), bf16[16,2,32,128]{3,2,1,0:T(8,128)(2,1)S(1)}, u32[]{:S(2)}, u32[]{:S(2)}) %all-to-all-start.5) | async-done | bytes 262176 | tf_op jit(solution)/shard_map/all_to_all | solution.py:21
  102.8 3.9 %all-to-all-start.3 = ((bf16[32,16,256]{2,1,0:T(8,128)(2,1)}), bf16[32,16,256]{2,1,0:T(8,128)(2,1)S(1)}, u32[]{:S(2)}, u32[]{:S(2)}) async-start(bf16[32,16,256]{2,1,0:T(8,128)(2,1)} %pad_maximum_fusion.1), calls=%async_computation.3 | async-start | bytes 524288 | tf_op jit(solution)/shard_map/all_to_all | solution.py:21
  107.2 11.7 %all-to-all-done.3 = bf16[32,16,256]{2,1,0:T(8,128)(2,1)S(1)} async-done(((bf16[32,16,256]{2,1,0:T(8,128)(2,1)}), bf16[32,16,256]{2,1,0:T(8,128)(2,1)S(1)}, u32[]{:S(2)}, u32[]{:S(2)}) %all-to-all-start.3) | async-done | bytes 262176 | tf_op jit(solution)/shard_map/all_to_all | solution.py:21
  121.6 0.6 slice.105
  122.2 4.3 %all-to-all-start.6 = ((bf16[32,16,128]{2,1,0:T(8,128)(2,1)}), bf16[32,16,128]{2,1,0:T(8,128)(2,1)S(1)}, u32[]{:S(2)}, u32[]{:S(2)}) async-start(bf16[32,16,128]{2,1,0:T(8,128)(2,1)} %bitcast.37), calls=%async_computation.6 | async-start | bytes 262144 | tf_op jit(solution)/shard_map/all_to_all | solution.py:21
  126.8 9.0 %all-to-all-done.6 = bf16[32,16,128]{2,1,0:T(8,128)(2,1)S(1)} async-done(((bf16[32,16,128]{2,1,0:T(8,128)(2,1)}), bf16[32,16,128]{2,1,0:T(8,128)(2,1)S(1)}, u32[]{:S(2)}, u32[]{:S(2)}) %all-to-all-start.6) | async-done | bytes 131104 | tf_op jit(solution)/shard_map/all_to_all | solution.py:21
  136.2 9.7 %all_to_all.70 = bf16[8,16,256]{2,1,0:T(8,128)(2,1)S(1)} all-to-all(bf16[8,16,256]{2,1,0:T(8,128)(2,1)S(1)} %bitcast.135), channel_id=1, replica_groups=mesh['z'=8,'x'=4,'y'=8,'c'=2] {'x','c'}, dimensions={0} | all-to-all | bytes 131072 | tf_op jit(solution)/shard_map/all_to_all | solution.py:21
  145.9 13.1 %all_to_all.71 = bf16[8,64,256]{2,1,0:T(8,128)(2,1)S(1)} all-to-all(bf16[8,64,256]{2,1,0:T(8,128)(2,1)S(1)} %broadcast_in_dim.227), channel_id=1, replica_groups=mesh['z'=8,'x'=4,'y'=8,'c'=2] {'y'}, dimensions={0} | all-to-all | bytes 524288 | tf_op jit(solution)/shard_map/all_to_all | solution.py:21
  159.4 17.6 %all_to_all.72 = bf16[32,16,512]{2,1,0:T(8,128)(2,1)S(1)} all-to-all(bf16[32,16,512]{2,1,0:T(8,128)(2,1)S(1)} %bitcast.122), channel_id=1, replica_groups=mesh['z'=8,'x'=4,'y'=8,'c'=2] {'z','x'}, dimensions={0} | all-to-all | bytes 1048576 | tf_op jit(solution)/shard_map/all_to_all | solution.py:21
  177.2 20.7 %all_to_all.73 = bf16[32,16,512]{2,1,0:T(8,128)(2,1)S(1)} all-to-all(bf16[32,16,512]{2,1,0:T(8,128)(2,1)S(1)} %broadcast_in_dim.228), channel_id=1, replica_groups=mesh['z'=8,'x'=4,'y'=8,'c'=2] {'z','x'}, dimensions={0} | all-to-all | bytes 1048576 | tf_op jit(solution)/shard_map/all_to_all | solution.py:21
  200.0 35.7 %all_to_all.74 = bf16[16,32,1024]{2,1,0:T(8,128)(2,1)S(1)} all-to-all(bf16[16,32,1024]{2,1,0:T(8,128)(2,1)S(1)} %bitcast.120), channel_id=1, replica_groups=mesh['z'=8,'x'=4,'y'=8,'c'=2] {'y','c'}, dimensions={0} | all-to-all | bytes 2097152 | tf_op jit(solution)/shard_map/all_to_all | solution.py:21
  236.3 20.0 %all_to_all.75 = bf16[16,32,448]{2,1,0:T(8,128)(2,1)S(1)} all-to-all(bf16[16,32,448]{2,1,0:T(8,128)(2,1)S(1)} %broadcast_in_dim.229), channel_id=1, replica_groups=mesh['z'=8,'x'=4,'y'=8,'c'=2] {'y','c'}, dimensions={0} | all-to-all | bytes 917504 | tf_op jit(solution)/shard_map/all_to_all | solution.py:21
  256.3 1.2 convolution_convert_fusion
  257.6 4.3 %all-to-all-start.13 = ((bf16[32,16,512]{2,1,0:T(8,128)(2,1)}), bf16[32,16,512]{2,1,0:T(8,128)(2,1)S(1)}, u32[]{:S(2)}, u32[]{:S(2)}) async-start(bf16[32,16,512]{2,1,0:T(8,128)(2,1)} %bitcast.51), calls=%async_computation.13 | async-start | bytes 1048576 | tf_op jit(solution)/shard_map/all_to_all | solution.py:21
  262.5 16.5 %all-to-all-done.13 = bf16[32,16,512]{2,1,0:T(8,128)(2,1)S(1)} async-done(((bf16[32,16,512]{2,1,0:T(8,128)(2,1)}), bf16[32,16,512]{2,1,0:T(8,128)(2,1)S(1)}, u32[]{:S(2)}, u32[]{:S(2)}) %all-to-all-start.13) | async-done | bytes 524320 | tf_op jit(solution)/shard_map/all_to_all | solution.py:21
  (152 shorter events, 13.0 us)
Async XLA Ops:
  0.6 255.7 %copy-start = (bf16[448,512]{1,0:T(8,128)(2,1)S(1)}, bf16[448,512]{1,0:T(8,128)(2,1)}, u32[]{:S(2)}) copy-start(bf16[448,512]{1,0:T(8,128)(2,1)} %param.25) | copy-start | bytes 1376260
  0.6 16.3 %copy-start.10 = (bf16[512,64]{0,1:T(8,128)(2,1)S(1)}, bf16[512,64]{0,1:T(8,128)(2,1)}, u32[]{:S(2)}) copy-start(bf16[512,64]{0,1:T(8,128)(2,1)} %param.21) | copy-start | bytes 196612
  0.7 17.0 %copy-start.8 = (s32[256]{0:T(256)S(1)}, s32[256]{0:T(256)}, u32[]{:S(2)}) copy-start(s32[256]{0:T(256)} %param.17) | copy-start | bytes 3076
  0.7 17.7 %copy-start.4 = (bf16[8,8,1024]{2,1,0:T(8,128)(2,1)S(1)}, bf16[8,8,1024]{2,1,0:T(8,128)(2,1)}, u32[]{:S(2)}) copy-start(bf16[8,8,1024]{2,1,0:T(8,128)(2,1)} %param.16) | copy-start | bytes 393220
  0.7 17.6 %copy-start.5 = (bf16[8,8,1024]{2,1,0:T(8,128)(2,1)S(1)}, bf16[8,8,1024]{2,1,0:T(8,128)(2,1)}, u32[]{:S(2)}) copy-start(bf16[8,8,1024]{2,1,0:T(8,128)(2,1)} %param.15) | copy-start | bytes 393220
  3.1 30.4 %copy-start.6 = (f32[512]{0:T(512)S(1)}, f32[512]{0:T(512)}, u32[]{:S(2)}) copy-start(f32[512]{0:T(512)} %param.18) | copy-start | bytes 6148
  3.1 30.1 %all-to-all-start = ((bf16[32,16,512]{2,1,0:T(8,128)(2,1)}), bf16[32,16,512]{2,1,0:T(8,128)(2,1)S(1)}, u32[]{:S(2)}, u32[]{:S(2)}) async-start(bf16[32,16,512]{2,1,0:T(8,128)(2,1)} %broadcast_in_dim.200), calls=%async_computation | async-start | bytes 1048576 | tf_op jit(solution)/shard_map/all_to_all | solution.py:21
  16.9 3.2 %collective-permute-start = (bf16[512,64]{0,1:T(8,128)(2,1)S(1)}, bf16[512,64]{0,1:T(8,128)(2,1)S(1)}, u32[]{:S(2)}, u32[]{:S(2)}) collective-permute-start(bf16[512,64]{0,1:T(8,128)(2,1)S(1)} %copy-done.10), channel_id=1, source_target_pairs={{0,0},{16,16},{32,64},{48,80},{64,128},{80,144},{96,192},{112,208}... | collective-permute-start | bytes 196616 | tf_op jit(solution)/shard_map/ppermute | solution.py:130
  18.4 15.1 %copy-start.9 = (bf16[512,256]{1,0:T(8,128)(2,1)S(1)}, bf16[512,256]{1,0:T(8,128)(2,1)}, u32[]{:S(2)}) copy-start(bf16[512,256]{1,0:T(8,128)(2,1)} %param.20) | copy-start | bytes 786436
  35.0 24.6 %all-to-all-start.1 = ((bf16[16,32,384]{2,1,0:T(8,128)(2,1)}), bf16[16,32,384]{2,1,0:T(8,128)(2,1)S(1)}, u32[]{:S(2)}, u32[]{:S(2)}) async-start(bf16[16,32,384]{2,1,0:T(8,128)(2,1)} %bitcast.10), calls=%async_computation.1 | async-start | bytes 786432 | tf_op jit(solution)/shard_map/all_to_all | solution.py:21
  59.6 18.3 %all-to-all-start.4 = ((bf16[8,2,8,8,128]{4,3,2,1,0:T(8,128)(2,1)}), bf16[8,2,8,8,128]{4,3,2,1,0:T(8,128)(2,1)S(1)}, u32[]{:S(2)}, u32[]{:S(2)}) async-start(bf16[8,2,8,8,128]{4,3,2,1,0:T(8,128)(2,1)} %copy.132), calls=%async_computation.4 | async-start | bytes 524288 | tf_op jit(solution)/shard_map/all_to_all | solution.py:21
  78.4 8.4 %all-to-all-start.2 = ((bf16[8,8,320]{2,1,0:T(8,128)(2,1)}), bf16[8,8,320]{2,1,0:T(8,128)(2,1)S(1)}, u32[]{:S(2)}, u32[]{:S(2)}) async-start(bf16[8,8,320]{2,1,0:T(8,128)(2,1)} %bitcast.12), calls=%async_computation.2 | async-start | bytes 98304 | tf_op jit(solution)/shard_map/all_to_all | solution.py:21
  86.9 15.9 %all-to-all-start.5 = ((bf16[16,2,32,128]{3,2,1,0:T(8,128)(2,1)}), bf16[16,2,32,128]{3,2,1,0:T(8,128)(2,1)S(1)}, u32[]{:S(2)}, u32[]{:S(2)}) async-start(bf16[16,2,32,128]{3,2,1,0:T(8,128)(2,1)} %bitcast.31), calls=%async_computation.5 | async-start | bytes 524288 | tf_op jit(solution)/shard_map/all_to_all | solution.py:21
  102.8 16.1 %all-to-all-start.3 = ((bf16[32,16,256]{2,1,0:T(8,128)(2,1)}), bf16[32,16,256]{2,1,0:T(8,128)(2,1)S(1)}, u32[]{:S(2)}, u32[]{:S(2)}) async-start(bf16[32,16,256]{2,1,0:T(8,128)(2,1)} %pad_maximum_fusion.1), calls=%async_computation.3 | async-start | bytes 524288 | tf_op jit(solution)/shard_map/all_to_all | solution.py:21
  121.5 37.5 %copy-start.3 = (bf16[256,512]{1,0:T(8,128)(2,1)S(1)}, bf16[256,512]{1,0:T(8,128)(2,1)}, u32[]{:S(2)}) copy-start(bf16[256,512]{1,0:T(8,128)(2,1)} %param.22) | copy-start | bytes 786436
  122.2 13.7 %all-to-all-start.6 = ((bf16[32,16,128]{2,1,0:T(8,128)(2,1)}), bf16[32,16,128]{2,1,0:T(8,128)(2,1)S(1)}, u32[]{:S(2)}, u32[]{:S(2)}) async-start(bf16[32,16,128]{2,1,0:T(8,128)(2,1)} %bitcast.37), calls=%async_computation.6 | async-start | bytes 262144 | tf_op jit(solution)/shard_map/all_to_all | solution.py:21
  159.4 38.8 %copy-start.7 = (f32[512]{0:T(512)S(1)}, f32[512]{0:T(512)}, u32[]{:S(2)}) copy-start(f32[512]{0:T(512)} %param.19) | copy-start | bytes 6148
  177.1 21.2 %copy-start.1 = (bf16[512,448]{0,1:T(8,128)(2,1)S(1)}, bf16[512,448]{0,1:T(8,128)(2,1)}, u32[]{:S(2)}) copy-start(bf16[512,448]{0,1:T(8,128)(2,1)} %param.24) | copy-start | bytes 1376260
  197.9 1.0 copy-start.2
  257.6 21.4 %all-to-all-start.13 = ((bf16[32,16,512]{2,1,0:T(8,128)(2,1)}), bf16[32,16,512]{2,1,0:T(8,128)(2,1)S(1)}, u32[]{:S(2)}, u32[]{:S(2)}) async-start(bf16[32,16,512]{2,1,0:T(8,128)(2,1)} %bitcast.51), calls=%async_computation.13 | async-start | bytes 1048576 | tf_op jit(solution)/shard_map/all_to_all | solution.py:21

commit v2 on v1

v2 whole, which is shorter than its diff:
```python
import functools
import math

import jax
import jax.numpy as jnp
import numpy as np
from jax import lax
from jax.experimental import pallas as pl
from jax.experimental.pallas import tpu as pltpu
from jax.sharding import Mesh, PartitionSpec as P

NZ, NX, NY, NC = 8, 4, 8, 2
HD = 128
EPS = 1e-05
ROPE_BASE = 500000.0
DP = ("z", "x")
TENSOR = ("y", "c")
F32 = jnp.float32
BF16 = jnp.bfloat16
LOW = -1e30
MESH = pl.DeviceIdType.MESH


def dot(a, b):
    return jnp.dot(a, b, preferred_element_type=F32)


def tables(ancestors, block, half):
    anc = ancestors.reshape(NZ * NX, 8)
    earlier = jnp.tril(jnp.ones((8, 8), jnp.int32), -1)
    mine = lax.dynamic_index_in_dim(anc, block, 0, keepdims=False)
    mine_block, mine_half = mine // 8, (mine // 4) % 2
    quad = mine // 4
    rank = jnp.sum((quad[:, None] == quad[None, :]) * earlier, axis=1)
    place = (mine_block % NX) * NZ + mine_block // NX
    row = jnp.arange(512)[:, None]
    col = jnp.arange(128)[None, :]
    col_place, col_half, col_rank = (
        jnp.broadcast_to(v.reshape(1, 2, 1, 4), (8, 2, 2, 4)).reshape(1, 128)
        for v in (place, mine_half, rank)
    )
    hit = (
        (col // 16 == row // 2 % 8)
        & ((col // 4) % 2 == 1)
        & (col_place == row // 16)
        & (col_half == half)
        & (col_rank == row % 2)
    )
    select = hit.astype(BF16)
    wanted = anc // 4 == block * 2 + half
    order = jnp.sum(wanted[:, None, :] * earlier[None], axis=2)
    which = jnp.stack(
        [jnp.sum(jnp.where(wanted & (order == s), anc % 4, 0), axis=1) for s in range(2)], axis=1
    )
    which = which.reshape(NZ, NX, 1, 2).transpose(1, 0, 2, 3)
    which = jnp.broadcast_to(which, (NX, NZ, 8, 2)).reshape(512, 1)
    own = jnp.arange(128)[:, None] % 4
    return select, select.T, jnp.concatenate([which, own], axis=0).astype(jnp.int32)


def angles(context):
    freq = np.power(np.float32(ROPE_BASE), -2.0 * np.arange(HD // 2, dtype=np.float32) / HD)
    freq = freq.astype(np.float32)
    step = (np.arange(16) // 4) % 2
    angle = (np.float32(context) + step.astype(np.float32))[:, None] * freq[None, :]
    cos, sin = np.cos(angle), np.sin(angle)
    both = np.stack([np.concatenate([cos, cos], 1), np.concatenate([-sin, sin], 1)])
    return jnp.asarray(both.astype(np.float32))


def iota(shape, dim):
    return lax.broadcasted_iota(jnp.int32, shape, dim)


def kernel(
    xrow, select, select_t, which, attn_gain, ffn_gain, rope, ck, cv, wq, wkv, wo, wg, wu, wd,
    attn_out, ffn_out,
    wq_v, wkv_r, wkv_p, wo_v, wg_r, wu_r, wgu_v, wd_v,
    ga, gg, part, bcs, bcr, bys, byr, cs, cr, cache1, cache2,
    ds_, dr, rs, rr, es, er, mb, fxs, fxr, fzs, fzr, ixs, ixr, izs, izr,
    hown, hcs, hcr, hys, hyr, hid,
    lsem, kvsem, gaz, gax, ggz, ggx, bc, by, csem, c1, c2, dsem, rsem, esem, e2sem,
    fx, fz, ix, iz, hc, hy, h2y, h2c,
):
    z, x, y, c = (lax.axis_index(a) for a in ("z", "x", "y", "c"))
    width = xrow.shape[1] * NY * NC
    ff = wg.shape[1]
    finals = []

    def loop(low, high, body):
        def step(k, carry):
            body(k)
            return carry

        lax.fori_loop(low, high, step, 0)

    def remote(src, dst, sems, n, **where):
        return pltpu.make_async_remote_copy(
            src_ref=src, dst_ref=dst, send_sem=sems.at[0, n], recv_sem=sems.at[1, n],
            device_id=where, device_id_type=MESH,
        )

    def arrived(ref, sems, n):
        pltpu.make_async_copy(ref, ref, sems.at[1, n]).wait()

    def sent(ref, sems, n):
        pltpu.make_async_copy(ref, ref, sems.at[0, n]).wait()

    zk = lambda k: lax.rem(z + k, NZ)
    zb = lambda k: lax.rem(z + NZ - k, NZ)
    xk = lambda j: lax.rem(x + j, NX)
    xb = lambda j: lax.rem(x + NX - j, NX)
    yk = lambda k: lax.rem(y + k, NY)
    yb = lambda k: lax.rem(y + NY - k, NY)

    loads = [
        pltpu.make_async_copy(wq, wq_v, lsem.at[0]),
        pltpu.make_async_copy(wo, wo_v, lsem.at[1]),
        pltpu.make_async_copy(wg, wg_r, lsem.at[2]),
        pltpu.make_async_copy(wu, wu_r, lsem.at[3]),
        pltpu.make_async_copy(wd, wd_v.at[pl.ds(0, ff)], lsem.at[4]),
        pltpu.make_async_copy(ck.at[:, pl.ds(pl.multiple_of(z * HD, HD), HD)], cache1.at[z, 0], lsem.at[5]),
        pltpu.make_async_copy(cv.at[:, pl.ds(pl.multiple_of(z * HD, HD), HD)], cache1.at[z, 1], lsem.at[6]),
    ]
    for load in loads:
        load.start()
    ga[x, z] = xrow[...]

    me = z * NX + x
    to_z, to_x = (me % 16) // 2, me // 16 * 2 + me % 2
    from_dp = x // 2 * 16 + 2 * z + x % 2
    from_z, from_x = from_dp // NX, from_dp % NX
    stays = from_dp == me
    barrier = pltpu.get_barrier_semaphore()

    def greet(**where):
        pl.semaphore_signal(barrier, inc=1, device_id=where, device_id_type=MESH)

    loop(1, 8, lambda k: greet(z=zk(k)))
    loop(1, 32, lambda n: greet(x=xk(n // 8), y=yk(n % 8)))
    loop(0, 4, lambda j: greet(x=xk(j), c=1 - c))
    loop(1, 8, lambda k: greet(y=yk(k), c=1 - c))

    @pl.when(jnp.logical_not(stays))
    def _():
        greet(z=to_z, x=to_x)
        greet(z=from_z, x=from_x)

    pl.semaphore_wait(barrier, jnp.where(stays, 49, 51))

    def gather_begin(buf, zs, xs):
        loop(1, 8, lambda k: remote(buf.at[x, z], buf.at[x, z], zs, k, z=zk(k)).start())
        loop(1, 4, lambda j: remote(buf.at[x, z], buf.at[x, z], xs, j, x=xk(j)).start())

    def gather_end(buf, zs, xs):
        def pass_on(k):
            block = buf.at[x, zb(k)]
            arrived(block, zs, k)
            loop(1, 4, lambda j: remote(block, block, xs, k * 4 + j, x=xk(j)).start())

        loop(1, 8, pass_on)
        loop(0, 8, lambda k: loop(1, 4, lambda j: arrived(buf.at[xb(j), zb(k)], xs, k * 4 + j)))

        def close():
            loop(1, 8, lambda k: sent(buf.at[x, z], zs, k))
            loop(0, 8, lambda k: loop(1, 4, lambda j: sent(buf.at[x, z], xs, k * 4 + j)))

        finals.append(close)

    def scatter_dp(xsend, xrecv, zsend, zrecv, xs, zs):
        def out(k):
            loop(1, 4, lambda j: remote(
                xsend.at[xk(j), zk(k + 1)], xrecv.at[x, zk(k + 1)], xs, lax.rem(k + 1, 8) * 4 + j, x=xk(j)
            ).start())

        loop(0, 8, out)

        def total(k):
            block = xsend[x, zk(k)].astype(F32)
            for j in range(1, 4):
                arrived(xrecv.at[xb(j), zk(k)], xs, k * 4 + j)
                block = block + xrecv[xb(j), zk(k)].astype(F32)
            return block

        def pass_on(k):
            zsend[zk(k)] = total(k).astype(BF16)
            remote(zsend.at[zk(k)], zrecv.at[z], zs, k, z=zk(k)).start()

        loop(1, 8, pass_on)
        acc = total(0)
        for k in range(1, 8):
            arrived(zrecv.at[zb(k)], zs, k)
            acc = acc + zrecv[zb(k)].astype(F32)

        def close():
            loop(0, 8, lambda k: loop(1, 4, lambda j: sent(xsend.at[0, 0], xs, k * 4 + j)))
            loop(1, 8, lambda k: sent(zsend.at[0], zs, k))

        finals.append(close)
        return acc

    def scatter_tensor(own, csend, crecv, ysend, yrecv, cs_, ys_, between):
        def pass_on(k):
            n = yk(k)
            arrived(crecv.at[n], cs_, k)
            ysend[n] = (own(n) + crecv[n].astype(F32)).astype(BF16)
            remote(ysend.at[n], yrecv.at[y], ys_, k, y=n).start()

        loop(1, 8, pass_on)
        arrived(crecv.at[y], cs_, 0)
        between()
        acc = own(y) + crecv[y].astype(F32)
        for k in range(1, 8):
            arrived(yrecv.at[yb(k)], ys_, k)
            acc = acc + yrecv[yb(k)].astype(F32)

        def close():
            loop(0, 8, lambda k: sent(csend.at[0], cs_, k))
            loop(1, 8, lambda k: sent(ysend.at[0], ys_, k))

        finals.append(close)
        return acc

    gather_begin(ga, gaz, gax)

    @pl.when(stays)
    def _():
        pltpu.make_async_copy(wkv, wkv_r, kvsem.at[1, 0]).start()

    @pl.when(jnp.logical_not(stays))
    def _():
        remote(wkv, wkv_r, kvsem, 0, z=to_z, x=to_x).start()

    def cache_out(k):
        cols = pl.ds(pl.multiple_of(zk(k) * HD, HD), HD)
        remote(ck.at[:, cols], cache1.at[z, 0], c1, k, z=zk(k)).start()
        remote(cv.at[:, cols], cache1.at[z, 1], c1, 8 + k, z=zk(k)).start()

    loop(1, 8, cache_out)

    wd_v[pl.ds(ff, 512 - ff), :] = jnp.zeros((512 - ff, 512), BF16)
    wgu_v[...] = jnp.zeros_like(wgu_v)
    wkv_p[...] = jnp.zeros_like(wkv_p)
    loads[2].wait()
    loads[3].wait()
    wgu_v[:, 0:ff] = wg_r[...]
    wgu_v[:, 512 : 512 + ff] = wu_r[...]
    gather_end(ga, gaz, gax)
    loads[0].wait()
    arrived(wkv_r, kvsem, 0)
    wkv_p[:, 0:64] = wkv_r[...]

    lane = iota((128, 128), 1)

    def squares_of(wide):
        square = jnp.sum(wide * wide, axis=1, keepdims=True)
        hi = square.astype(BF16).astype(F32)
        return jnp.where(lane == 64, hi, 0.0) + jnp.where(lane == 65, square - hi, 0.0)

    def project(n):
        wide = ga[n].reshape(128, 512).astype(F32)
        scaled = (wide * attn_gain[...]).astype(BF16)
        part[n, :, :, :, 0:256] = dot(scaled, wq_v[...]).reshape(8, 2, 8, 256)
        part[n, :, :, :, 256:384] = (dot(scaled, wkv_p[...]) + squares_of(wide)).reshape(8, 2, 8, 128)

    loop(0, 4, project)

    def to_core(k):
        n = yk(k + 1)
        bcs[n] = part[:, n, 1 - c].reshape(32, 384).astype(BF16)
        remote(bcs.at[n], bcr.at[n], bc, lax.rem(k + 1, 8), c=1 - c).start()

    loop(0, 8, to_core)

    def cache_pass():
        loads[5].wait()
        loads[6].wait()

        def came(k):
            arrived(cache1.at[zb(k), 0], c1, k)
            arrived(cache1.at[zb(k), 1], c1, 8 + k)

        loop(1, 8, came)
        other = 1 - c
        keep = pltpu.make_async_copy(
            cache1.at[y, :, pl.ds(pl.multiple_of(c * 32, 32), 32), :], cache2.at[y * 2 + c], lsem.at[7]
        )
        keep.start()

        def pass_same(k):
            remote(
                cache1.at[yk(k), :, pl.ds(pl.multiple_of(c * 32, 32), 32), :], cache2.at[y * 2 + c],
                c2, k, y=yk(k),
            ).start()

        loop(1, 8, pass_same)

        def pass_other(k):
            remote(
                cache1.at[yk(k), :, pl.ds(pl.multiple_of(other * 32, 32), 32), :], cache2.at[y * 2 + c],
                c2, 8 + k, y=yk(k), c=other,
            ).start()

        loop(0, 8, pass_other)
        keep.wait()

        def close():
            loop(1, 8, lambda k: sent(cache1.at[0, 0], c1, k))
            loop(1, 8, lambda k: sent(cache1.at[0, 0], c1, 8 + k))
            loop(1, 16, lambda k: sent(cache2.at[0], c2, k))

            @pl.when(jnp.logical_not(stays))
            def _():
                sent(wkv_r, kvsem, 0)

        finals.append(close)

    acc = scatter_tensor(
        lambda n: part[:, n, c].reshape(32, 384), bcs, bcr, bys, byr, bc, by, cache_pass
    )
    factor = lax.rsqrt((acc[:, 320:321] + acc[:, 321:322]) / width + EPS)
    cs[...] = (acc * factor).astype(BF16).astype(F32).reshape(4, 8, 384)

    def share(src, dst, sems):
        def one(n):
            j, e = n // 2, n % 2
            to_c = lax.rem(c + e, 2)
            remote(src.at[xk(j)], dst.at[x, c], sems, n, x=xk(j), c=to_c).start()

        dst[x, c] = src[x]
        loop(1, 8, one)
        loop(1, 8, lambda n: arrived(dst.at[xb(n // 2), lax.rem(c + n % 2, 2)], sems, n))
        finals.append(lambda: loop(1, 8, lambda n: sent(src.at[0], sems, n)))

    share(cs, cr, csem)

    def rotated(rows):
        count = rows.shape[0] // 16
        cos = jnp.concatenate([rope[0]] * count, axis=0)
        sin = jnp.concatenate([rope[1]] * count, axis=0)
        return (rows * cos + pltpu.roll(rows, 64, 1) * sin).astype(BF16)

    heads = [cr[n].reshape(16, 384) for n in range(4)]
    queries = rotated(
        jnp.concatenate([h[:, a : a + HD] for h in heads for a in (0, HD)], axis=0)
    )
    low = iota((16, HD), 1) < 64
    join = lambda a, b: jnp.where(low, a[:, 256:384], pltpu.roll(b[:, 256:384], 64, 1))
    new_keys = rotated(join(heads[0], heads[1]))
    new_values = join(heads[2], heads[3]).astype(BF16)

    spot = x * 8 + y
    pairs = jnp.concatenate([new_keys, new_values, jnp.zeros((96, HD), BF16)], axis=0)
    ds_[:, :, 0:HD] = dot(select[...], queries).astype(BF16).reshape(32, 16, HD)
    ds_[:, :, HD : 2 * HD] = dot(select[...], pairs).astype(BF16).reshape(32, 16, HD)
    dr[spot] = ds_[spot]

    def trade(src, dst, sems):
        def one(n):
            px, py = xk(n // 8), yk(n % 8)
            remote(src.at[px * 8 + py], dst.at[spot], sems, n, x=px, y=py).start()

        loop(1, 32, one)
        finals.append(lambda: loop(1, 32, lambda n: sent(src.at[0], sems, n)))

    def traded(dst, sems):
        loop(1, 32, lambda n: arrived(dst.at[xb(n // 8) * 8 + yb(n % 8)], sems, n))

    trade(ds_, dr, dsem)
    loop(1, 16, lambda k: arrived(cache2.at[yb(lax.rem(k, 8)) * 2 + lax.rem(c + k // 8, 2)], c2, k))
    traded(dr, dsem)

    row = iota((512, 512), 0)
    col = iota((512, 512), 1)
    same = (row // 16 == col // 16) & (row % 2 == col % 2)
    kind = col // 2 % 8
    tail = dr[:, :, HD : 2 * HD].reshape(512, HD)
    own_key = dot(jnp.where(same & (kind == 0), 1.0, 0.0).astype(BF16), tail)
    own_value = dot(jnp.where(same & (kind == 1), 1.0, 0.0).astype(BF16), tail)
    asked = jnp.concatenate([dr[:, :, 0:HD].reshape(512, HD), queries], axis=0)
    pad = jnp.zeros((112, HD), BF16)
    keys = jnp.concatenate([cache2[:, 0].reshape(512, HD), new_keys, pad], axis=0)
    values = jnp.concatenate([cache2[:, 1].reshape(512, HD), new_values, pad], axis=0)
    scale = 1.0 / math.sqrt(HD)
    scores = lax.dot_general(asked, keys, (((1,), (1,)), ((), ())), preferred_element_type=F32)
    k = iota((1, 640), 1)
    new = k - 512
    key_particle = jnp.where(k < 512, (k // 8) % 4, k % 4)
    key_ok = (k < 512) | ((new < 16) & ((new // 4) % 2 == 0) & (new // 8 == c))
    key_particle = jnp.where(key_ok, key_particle, -1)
    scores = jnp.where(key_particle == which[...], scores * scale, LOW)
    own = jnp.sum(asked[0:512].astype(F32) * own_key, axis=1, keepdims=True) * scale
    own = jnp.concatenate([own, jnp.full((128, 1), LOW, F32)], axis=0)
    highest = jnp.maximum(jnp.max(scores, axis=1, keepdims=True), own)
    weights = jnp.exp(scores - highest)
    own = jnp.exp(own - highest)
    totals = jnp.sum(weights, axis=1, keepdims=True) + own
    mixed = dot(weights.astype(BF16), values)
    extra = jnp.concatenate([own[0:512] * own_value, jnp.zeros((128, HD), F32)], axis=0)
    mixed = (mixed + extra) / totals

    rs[...] = mixed[0:512].astype(BF16).reshape(32, 16, HD)
    rr[spot] = rs[spot]
    trade(rs, rr, rsem)
    r = iota((128, 1), 0)
    first = jnp.where(((r // 4) % 2 == 0) & ((r // 8) % 2 == c), mixed[512:640], 0.0)
    traded(rr, rsem)
    both = (first + dot(select_t[...], rr[...].reshape(512, HD))).astype(BF16)
    for n in range(4):
        es[n, :, 0:HD] = both[n * 32 : n * 32 + 16]
        es[n, :, HD : 2 * HD] = both[n * 32 + 16 : n * 32 + 32]
    share(es, er, esem)
    mb[y] = (er[:, 0].astype(F32) + er[:, 1].astype(F32)).astype(BF16).reshape(64, 256)
    loop(1, 8, lambda k: remote(mb.at[y], mb.at[y], e2sem, k, y=yk(k)).start())
    finals.append(lambda: loop(1, 8, lambda k: sent(mb.at[0], e2sem, k)))
    loads[1].wait()
    loop(1, 8, lambda k: arrived(mb.at[yb(k)], e2sem, k))

    for n in range(4):
        rows = mb[:, n * 16 : n * 16 + 16, :].reshape(128, 256)
        fxs[n] = dot(rows, wo_v[...]).astype(BF16).reshape(8, 16, 512)
    attn = scatter_dp(fxs, fxr, fzs, fzr, fx, fz).astype(BF16)
    attn_out[...] = attn
    gg[x, z] = (xrow[...].astype(F32) + attn.astype(F32)).astype(BF16)

    gather_begin(gg, ggz, ggx)
    gather_end(gg, ggz, ggx)

    def gate_up(n):
        wide = gg[n].reshape(128, 512).astype(F32)
        scaled = (wide * ffn_gain[...]).astype(BF16)
        return dot(scaled, wgu_v[...]), squares_of(wide)

    for n in range(2):
        value, square = gate_up(2 * (1 - c) + n)
        at = slice(n * 16, n * 16 + 16)
        hcs[:, at, :] = value.astype(BF16).reshape(8, 16, 1024)
        hcs[:, at, 384:512] = (value[:, 384:512] + square).astype(BF16).reshape(8, 16, 128)

    def to_core_again(k):
        n = yk(k + 1)
        remote(hcs.at[n], hcr.at[n], hc, lax.rem(k + 1, 8), c=1 - c).start()

    loop(0, 8, to_core_again)
    for n in range(2):
        value, square = gate_up(2 * c + n)
        at = slice(n * 16, n * 16 + 16)
        hown[:, at, :] = value.reshape(8, 16, 1024)
        hown[:, at, 384:512] = (value[:, 384:512] + square).reshape(8, 16, 128)
    acc = scatter_tensor(lambda n: hown[n], hcs, hcr, hys, hyr, hc, hy, lambda: None)
    factor = lax.rsqrt((acc[:, ff : ff + 1] + acc[:, ff + 1 : ff + 2]) / width + EPS)
    gate, up = acc[:, 0:512] * factor, acc[:, 512:1024] * factor
    hidden = gate / (1.0 + jnp.exp(-gate)) * up
    hid[c, y] = jnp.where(iota((32, 512), 1) < ff, hidden, 0.0).astype(BF16)

    loop(1, 8, lambda k: remote(hid.at[c, y], hid.at[c, y], h2y, k, y=yk(k)).start())
    remote(hid.at[c, y], hid.at[c, y], h2c, 0, c=1 - c).start()

    def pass_hidden(k):
        block = hid.at[c, yb(k)]
        arrived(block, h2y, k)
        remote(block, block, h2c, k, c=1 - c).start()

    loop(1, 8, pass_hidden)
    loads[4].wait()
    loop(0, 8, lambda k: arrived(hid.at[1 - c, yb(k)], h2c, k))

    for n in range(4):
        rows = hid[n // 2, :, (n % 2) * 16 : (n % 2) * 16 + 16, :].reshape(128, 512)
        ixs[n] = dot(rows, wd_v[...]).astype(BF16).reshape(8, 16, 512)
    ffn_out[...] = scatter_dp(ixs, ixr, izs, izr, ix, iz).astype(BF16)

    loop(1, 8, lambda k: sent(hid.at[0, 0], h2y, k))
    loop(0, 8, lambda k: sent(hid.at[0, 0], h2c, k))
    for close in finals:
        close()


def local(
    x_first, x_second, cache_keys, cache_values, ancestors, attn_gain, ffn_gain,
    w_query, w_keyval, w_out, w_gate, w_up, w_down,
):
    z, x, y, c = (lax.axis_index(a) for a in ("z", "x", "y", "c"))
    context = cache_keys.shape[1] * NY * NC
    select, select_t, which = tables(ancestors, y * NX + x, c)
    rows = jnp.stack([x_first.reshape(2, 4, -1), x_second.reshape(2, 4, -1)], axis=1).reshape(16, -1)
    v = lambda *shape: pltpu.VMEM(shape, BF16)
    f = lambda *shape: pltpu.VMEM(shape, F32)
    sem = lambda n: pltpu.SemaphoreType.DMA((2, n))
    near, far = pl.BlockSpec(memory_space=pltpu.VMEM), pl.BlockSpec(memory_space=pl.ANY)
    big = [v(4, 8, 16, 512), v(4, 8, 16, 512), v(8, 16, 512), v(8, 16, 512)]
    attn, ffn = pl.pallas_call(
        kernel,
        out_shape=[jax.ShapeDtypeStruct((16, 512), BF16)] * 2,
        in_specs=[near] * 7 + [far] * 8,
        out_specs=[near, near],
        scratch_shapes=[
            v(512, 256), v(512, 64), v(512, 128), v(256, 512), v(512, 448), v(512, 448), v(512, 1024),
            v(512, 512),
            v(4, 8, 16, 512), v(4, 8, 16, 512), f(4, 8, 2, 8, 384),
            *[v(8, 32, 384)] * 4,
            f(4, 8, 384), f(4, 2, 8, 384), v(8, 2, 64, HD), v(16, 2, 32, HD),
            v(32, 16, 256), v(32, 16, 256), v(32, 16, HD), v(32, 16, HD),
            v(4, 16, 256), v(4, 2, 16, 256), v(8, 64, 256),
            *big, *big,
            f(8, 32, 1024), *[v(8, 32, 1024)] * 4, v(2, 8, 32, 512),
            pltpu.SemaphoreType.DMA((8,)), sem(1), sem(8), sem(32), sem(8), sem(32), sem(8), sem(8),
            sem(8), sem(16), sem(16), sem(32), sem(32), sem(8), sem(8),
            sem(32), sem(8), sem(32), sem(8), sem(8), sem(8), sem(8), sem(8),
        ],
        compiler_params=pltpu.CompilerParams(
            collective_id=0, has_side_effects=True, vmem_limit_bytes=48 * 2**20
        ),
        cost_estimate=pl.CostEstimate(flops=2**30, bytes_accessed=2**22, transcendentals=2**19),
    )(
        rows, select, select_t, which, attn_gain[None], ffn_gain[None], angles(context),
        cache_keys.reshape(64, -1), cache_values.reshape(64, -1),
        w_query, w_keyval, w_out, w_gate, w_up, w_down,
    )

    def by_step(block):
        return block.reshape(2, 2, 4, -1).transpose(1, 0, 2, 3).reshape(2, 8, -1)

    return by_step(attn), by_step(ffn)


def solution(mesh):
    fine = Mesh(mesh.devices.reshape(NZ, NX, NY, NC), ("z", "x", "y", "c"))
    rows, cols = P(TENSOR, DP), P(DP, TENSOR)
    return jax.shard_map(
        local,
        mesh=fine,
        in_specs=(
            cols, cols, P(DP, TENSOR, None), P(DP, TENSOR, None), P(), P(TENSOR), P(TENSOR),
            rows, rows, cols, rows, rows, cols,
        ),
        out_specs=(P(None, DP, TENSOR), P(None, DP, TENSOR)),
        check_vma=False,
    )
```

time: 281 us -> 154 us (0.55)
  Pallas kernels: 0 us -> 144 us
  blocking collectives: 117 us -> 0 us
  waiting for transfers between devices: 90.5 us -> 0 us
  starting transfers between devices: 50.6 us -> 0 us
  matrix products: 5.58 us -> 0 us
  local copies, waits for them, and re-layouts: 10.5 us -> 6.99 us
  other arithmetic: 4.19 us -> 0.89 us
    pallas_call x0 -> x1, Pallas kernels: none -> 144 us  [local(): pl.pallas_call(kernel, out_shape=[jax.ShapeDtypeStruct((16, 512), BF16)]...]
    all_to_all x6 -> x0, blocking collectives: 117 us -> none  [exchange(): return lax.all_to_all(blocks, axes, split_axis=0, concat_axis=0, tiled=True)]
    all_to_all x8 -> x0, waiting for transfers between devices: 90.5 us -> none  [exchange(): return lax.all_to_all(blocks, axes, split_axis=0, concat_axis=0, tiled=True)]
    all_to_all x8 -> x0, starting transfers between devices: 49.9 us -> none  [exchange(): return lax.all_to_all(blocks, axes, split_axis=0, concat_axis=0, tiled=True)]
    dot_general x12 -> x0, matrix products: 5.58 us -> none  [the longest x10 4.71 us: dot(): return jnp.dot(a, b, preferred_element_type=F32)]
    unnamed x25 -> x31, local copies, waits for them, and re-layouts: 1.58 us -> 4.39 us
  transfers between devices with their start and end apart: 9 -> 0, of which waited for: 8 -> 0; matrix products, arithmetic and copies ran while one was open for 2% -> 0% of each run, Pallas kernels for 0% -> 0%
where the time goes in v2:
time: 154 us; the launch traced here: 153 us
  Pallas kernels  144 us (94%)
  local copies, waits for them, and re-layouts  6.99 us (5%)
    pallas_call x1, Pallas kernels, local(): pl.pallas_call(kernel, out_shape=[jax.ShapeDtypeStruct((16, 512), BF16)]...  144 us
    unnamed x31, local copies, waits for them, and re-layouts  4.39 us

profile of v2, /device:TPU:1, one launch (start us, length us, event | category | flops | bytes accessed | tf_op | source)
XLA Modules:
  0.0 153.3 jit_solution(1279921306048489942)
XLA Ops:
  0.7 0.6 copy-done.11
  1.4 0.7 copy-done.12
  2.1 0.7 copy-done.13
  2.8 0.1 reshape.431
  2.9 0.1 copy.47
  2.9 0.1 squeeze.6
  3.1 0.2 fusion.5
  3.3 0.1 broadcast_in_dim.51
  3.4 0.1 multiply_reduce_fusion
  3.5 0.1 stack.13
  3.6 0.1 stack.14
  3.7 0.1 eq.146
  3.8 0.1 copy.52
  3.9 0.1 eq.151
  4.1 0.1 eq.140
  4.2 0.0 copy-start.10
  4.2 0.1 reshape.432
  4.4 0.2 and_convert_fusion.select_t
  4.5 0.3 and_convert_fusion.1.select
  4.8 0.2 copy-done.10
  5.0 0.1 copy.54.wkv
  5.1 0.2 copy.53.which
  5.4 0.0 copy-start.7
  5.4 0.2 copy.55.wg
  5.6 0.7 copy-done.9
  6.4 0.2 copy.56.wu
  6.6 0.8 copy-done
  7.4 0.1 copy-done.1
  7.5 0.1 copy-done.2
  7.5 144.5 %shard_map.149 = (bf16[16,512]{1,0:T(8,128)(2,1)S(1)}, bf16[16,512]{1,0:T(8,128)(2,1)S(1)}) custom-call(bf16[16,512]{1,0:T(8,128)(2,1)S(1)} %reshape.430.xrow, bf16[512,128]{1,0:T(8,128)(2,1)S(1)} %and_convert_fusion.1.select, bf16[128,512]{1,0:T(8,128)(2,1)S(1)} %and_convert_fusion.select_t, s32[640,1]{1,0:T(8,128)S(1)} %copy.53.which, ...), custom_call_target="tpu_custom_call" | custom-call | flops 1073741824 | bytes 4194304 | tf_op jit(solution)/shard_map/pallas_call | solution.py:492
  152.0 0.6 reshape.436
  152.7 0.6 reshape.438
  (43 shorter events, 0.3 us)
Async XLA Ops:
  0.6 0.7 copy-start.11
  1.3 0.7 copy-start.12
  2.1 0.7 copy-start.13
  4.2 0.8 copy-start.10
  4.2 1.1 copy-start.8
  5.3 1.0 copy-start.9
  5.3 1.2 copy-start.3
  5.4 1.2 copy-start.4
  5.4 1.2 copy-start.5
  5.4 1.2 copy-start.6
  5.4 1.2 copy-start.7
  6.4 1.0 copy-start
  6.4 1.1 copy-start.1
  6.4 1.2 copy-start.2

commit v3 on v2

v3 whole, which is shorter than its diff:
```python
import functools
import math

import jax
import jax.numpy as jnp
import numpy as np
from jax import lax
from jax.experimental import pallas as pl
from jax.experimental.pallas import tpu as pltpu
from jax.sharding import Mesh, PartitionSpec as P

NZ, NX, NY, NC = 8, 4, 8, 2
HD = 128
EPS = 1e-05
ROPE_BASE = 500000.0
DP = ("z", "x")
TENSOR = ("y", "c")
F32 = jnp.float32
BF16 = jnp.bfloat16
LOW = -1e30
VMEM_LIMIT = 63 * 2**20
MESH = pl.DeviceIdType.MESH


def dot(a, b):
    return jnp.dot(a, b, preferred_element_type=F32)


def angles(context):
    freq = np.power(np.float32(ROPE_BASE), -2.0 * np.arange(HD // 2, dtype=np.float32) / HD)
    freq = freq.astype(np.float32)
    step = (np.arange(16) // 4) % 2
    angle = (np.float32(context) + step.astype(np.float32))[:, None] * freq[None, :]
    cos, sin = np.cos(angle), np.sin(angle)
    both = np.stack([np.concatenate([cos, cos], 1), np.concatenate([-sin, sin], 1)])
    return jnp.asarray(both.astype(np.float32))


def iota(shape, dim):
    return lax.broadcasted_iota(jnp.int32, shape, dim)


def kernel(
    anc, x_first, x_second, attn_gain, ffn_gain, rope, ck, cv, wq, wkv, wo, wg, wu, wd,
    attn_out, ffn_out,
    xrow, select, select_t, local_row, wq_v, wkv_v, wo_v, wgu_v, wd_v,
    ga, gg, part, bcs, bcr, bys, byr, cs, cr, cache1, cache2,
    ds_, dr, rs, rr, es, er, mb, fxs, fxr, fzs, fzr, ixs, ixr, izs, izr,
    hown, hcs, hcr, hys, hyr, hid,
    lsem, kvsem, gaz, gax, ggz, ggx, bc, by, csem, c1, c2, dsem, rsem, esem, e2sem,
    fx, fz, ix, iz, hc, hy, h2y, h2c,
):
    z, x, y, c = (lax.axis_index(a) for a in ("z", "x", "y", "c"))
    width = x_first.shape[1] * NY * NC
    ff = wg.shape[0]
    finals = []

    def loop(low, high, body):
        def step(k, carry):
            body(k)
            return carry

        lax.fori_loop(low, high, step, 0)

    def remote(src, dst, sems, n, **where):
        return pltpu.make_async_remote_copy(
            src_ref=src, dst_ref=dst, send_sem=sems.at[0, 0], recv_sem=sems.at[1, n],
            device_id=where, device_id_type=MESH,
        )

    def arrived(ref, sems, n):
        pltpu.make_async_copy(ref, ref, sems.at[1, n]).wait()

    def sent(ref, sems):
        pltpu.make_async_copy(ref, ref, sems.at[0, 0]).wait()

    most = lambda ref, n: ref.at[pl.ds(0, n)]

    zk = lambda k: lax.rem(z + k, NZ)
    zb = lambda k: lax.rem(z + NZ - k, NZ)
    xk = lambda j: lax.rem(x + j, NX)
    xb = lambda j: lax.rem(x + NX - j, NX)
    yk = lambda k: lax.rem(y + k, NY)
    yb = lambda k: lax.rem(y + NY - k, NY)

    me = z * NX + x
    to_z, to_x = (me % 16) // 2, me // 16 * 2 + me % 2
    from_dp = x // 2 * 16 + 2 * z + x % 2
    from_z, from_x = from_dp // NX, from_dp % NX
    stays = from_dp == me
    barrier = pltpu.get_barrier_semaphore()

    def greet(**where):
        pl.semaphore_signal(barrier, inc=1, device_id=where, device_id_type=MESH)

    loop(1, 8, lambda k: greet(z=zk(k)))
    loop(1, 32, lambda n: greet(x=xk(n // 8), y=yk(n % 8)))
    loop(0, 4, lambda j: greet(x=xk(j), c=1 - c))
    loop(1, 8, lambda k: greet(y=yk(k), c=1 - c))

    @pl.when(jnp.logical_not(stays))
    def _():
        greet(z=to_z, x=to_x)
        greet(z=from_z, x=from_x)


    loads = [
        pltpu.make_async_copy(wq, wq_v, lsem.at[0]),
        pltpu.make_async_copy(wo, wo_v, lsem.at[1]),
        pltpu.make_async_copy(wg, wgu_v.at[pl.ds(0, ff)], lsem.at[2]),
        pltpu.make_async_copy(wu, wgu_v.at[pl.ds(512, ff)], lsem.at[3]),
        pltpu.make_async_copy(wd, wd_v.at[pl.ds(0, ff)], lsem.at[4]),
        pltpu.make_async_copy(ck.at[:, pl.ds(pl.multiple_of(z * HD, HD), HD)], cache1.at[z, 0], lsem.at[5]),
        pltpu.make_async_copy(cv.at[:, pl.ds(pl.multiple_of(z * HD, HD), HD)], cache1.at[z, 1], lsem.at[6]),
    ]
    for load in loads:
        load.start()
    r = iota((16, 16), 0)
    q = iota((16, 16), 1)
    order16 = jnp.where(q == (r // 4) % 2 * 8 + r // 8 * 4 + r % 4, 1.0, 0.0).astype(BF16)
    r_t, q_t = q, r
    back16 = jnp.where(q_t == (r_t // 4) % 2 * 8 + r_t // 8 * 4 + r_t % 4, 1.0, 0.0).astype(BF16)
    pair = jnp.concatenate([x_first[...].astype(F32), x_second[...].astype(F32)], axis=0)
    xrow[...] = dot(order16, pair.astype(BF16)).astype(BF16)
    ga[x, z] = xrow[...]

    pl.semaphore_wait(barrier, jnp.where(stays, 49, 51))

    def turn(i, first):
        return jnp.where(i == 0, 0, 1 + lax.rem(i + 6 + first, 7))

    def gather_begin(buf, zs, xs):
        block = buf.at[x, z]

        def one(i):
            k = turn(i, y)
            remote(block, block, zs, k, z=zk(k)).start()

        loop(1, 8, one)
        loop(1, 4, lambda j: remote(block, block, xs, 0, x=xk(j)).start())

    def dp_to_tensor(buf, zs, xs, work, own, csend, crecv, ysend, yrecv, cs_, ys_, also=None):
        def pass_on(i):
            k = turn(i, y)
            block = buf.at[x, zb(k)]
            arrived(block, zs, k)
            loop(1, 4, lambda j: remote(block, block, xs, k, x=xk(j)).start())

        def to_ring(i):
            n = zb(turn(i, y))
            arrived(crecv.at[n], cs_, n)

            @pl.when(n != y)
            def _():
                ysend[n] = (own(n) + crecv[n].astype(F32)).astype(BF16)
                remote(ysend.at[n], yrecv.at[y], ys_, 0, y=n).start()

        def body(i):
            k = turn(i, y)
            n = zb(k)
            pl.when(i < 6)(lambda: pass_on(i + 2))
            arrived(buf.at[pl.ds(0, 3), 0], xs, k)
            work(n)
            remote(csend.at[n], crecv.at[n], cs_, n, c=1 - c).start()
            pl.when(i >= 4)(lambda: to_ring(i - 4))
            if also is not None:
                pl.when(i == 4)(also)

        pass_on(1)
        loop(0, 8, body)
        loop(4, 8, to_ring)

        def close():
            sent(buf.at[0, pl.ds(0, 7)], zs)
            sent(most(buf, 3), xs)
            sent(csend, cs_)
            sent(most(ysend, 7), ys_)

        finals.append(close)

        def finish():
            acc = own(y) + crecv[y].astype(F32)
            arrived(most(yrecv, 7), ys_, 0)
            for k in range(1, 8):
                acc = acc + yrecv[yb(k)].astype(F32)
            return acc

        return finish

    def tensor_to_dp(ahead, work, xsend, xrecv, zsend, zrecv, xs, zs):
        def total(n):
            arrived(xrecv.at[pl.ds(0, 3), 0], xs, n)
            block = xsend[x, n].astype(F32)
            for j in range(1, 4):
                block = block + xrecv[xb(j), n].astype(F32)
            return block

        def to_ring(i):
            n = yb(turn(i, z))
            zsend[n] = total(n).astype(BF16)

            @pl.when(n != z)
            def _():
                remote(zsend.at[n], zrecv.at[z], zs, 0, z=n).start()

        def body(i):
            k = turn(i, z)
            n = yb(k)
            ahead(i, k, n)
            xsend[:, n] = work(n).astype(BF16).reshape(4, 16, 512)
            loop(1, 4, lambda j: remote(xsend.at[xk(j), n], xrecv.at[x, n], xs, n, x=xk(j)).start())
            pl.when(i >= 4)(lambda: to_ring(i - 4))

        loop(0, 8, body)
        loop(4, 8, to_ring)
        acc = zsend[z].astype(F32)
        arrived(most(zrecv, 7), zs, 0)
        for k in range(1, 8):
            acc = acc + zrecv[zb(k)].astype(F32)

        def close():
            sent(most(xsend, 3), xs)
            sent(most(zsend, 7), zs)

        finals.append(close)
        return acc

    gather_begin(ga, gaz, gax)

    @pl.when(stays)
    def _():
        pltpu.make_async_copy(wkv, wkv_v.at[pl.ds(0, 64)], kvsem.at[1, 0]).start()

    @pl.when(jnp.logical_not(stays))
    def _():
        remote(wkv, wkv_v.at[pl.ds(0, 64)], kvsem, 0, z=to_z, x=to_x).start()

    def cache_out(k):
        cols = pl.ds(pl.multiple_of(zk(k) * HD, HD), HD)
        remote(ck.at[:, cols], cache1.at[z, 0], c1, 0, z=zk(k)).start()
        remote(cv.at[:, cols], cache1.at[z, 1], c1, 0, z=zk(k)).start()

    loop(1, 8, cache_out)

    wd_v[pl.ds(ff, 512 - ff), :] = jnp.zeros((512 - ff, 512), BF16)
    wgu_v[pl.ds(ff, 512 - ff), :] = jnp.zeros((512 - ff, 512), BF16)
    wgu_v[pl.ds(512 + ff, 512 - ff), :] = jnp.zeros((512 - ff, 512), BF16)
    wkv_v[pl.ds(64, 64), :] = jnp.zeros((64, 512), BF16)
    mine = [anc[(y * NX + x) * 8 + p] for p in range(8)]
    codes = []
    for p in range(8):
        block = lax.shift_right_logical(mine[p], 3)
        place = (block & 3) * 8 + lax.shift_right_logical(block, 2)
        quad = lax.shift_right_logical(mine[p], 2)
        rank = jnp.int32(0)
        for other in range(p):
            rank = rank + jnp.where(lax.shift_right_logical(mine[other], 2) == quad, 1, 0)
        codes.append(place * 4 + (quad & 1) * 2 + rank)

    def per_particle(index, values):
        out = jnp.zeros(index.shape, jnp.int32)
        for p in range(8):
            out = jnp.where((index // 8) % 2 * 4 + index % 4 == p, values[p], out)
        return out

    def hits(row, col, code):
        hit = (col // 16 == row % 8) & ((col // 4) % 2 == 1)
        return jnp.where(hit & (code == row // 16 * 4 + c * 2 + row // 8 % 2), 1.0, 0.0).astype(BF16)

    select[...] = hits(iota((512, 128), 0), iota((512, 128), 1), per_particle(iota((1, 128), 1), codes))
    select_t[...] = hits(iota((128, 512), 1), iota((128, 512), 0), per_particle(iota((128, 1), 0), codes))
    spots = per_particle(iota((16, 128), 0), [m & 3 for m in mine])
    local_row[...] = spots.astype(F32).astype(BF16)
    loads[0].wait()
    arrived(wkv_v.at[pl.ds(0, 64)], kvsem, 0)

    lane = iota((64, 128), 1)

    def dot_t(a, b):
        return lax.dot_general(a, b, (((1,), (1,)), ((), ())), preferred_element_type=F32)

    def squares_of(wide):
        square = jnp.sum(wide * wide, axis=1, keepdims=True)
        hi = square.astype(BF16).astype(F32)
        return jnp.where(lane == 64, hi, 0.0) + jnp.where(lane == 65, square - hi, 0.0)

    def project(n):
        wide = ga[:, n].reshape(64, 512).astype(F32)
        scaled = (wide * attn_gain[...]).astype(BF16)
        part[n, :, :, :, 0:256] = dot(scaled, wq_v[...]).reshape(4, 2, 8, 256)
        part[n, :, :, :, 256:384] = (dot_t(scaled, wkv_v[...]) + squares_of(wide)).reshape(4, 2, 8, 128)
        bcs[n] = part[n, :, 1 - c].reshape(32, 384).astype(BF16)

    def cache_pass():
        loads[5].wait()
        loads[6].wait()

        arrived(most(cache1, 7), c1, 0)
        other = 1 - c
        keep = pltpu.make_async_copy(
            cache1.at[y, :, pl.ds(pl.multiple_of(c * 32, 32), 32), :], cache2.at[y * 2 + c], lsem.at[7]
        )
        keep.start()

        def pass_same(k):
            remote(
                cache1.at[yk(k), :, pl.ds(pl.multiple_of(c * 32, 32), 32), :], cache2.at[y * 2 + c],
                c2, 0, y=yk(k),
            ).start()

        loop(1, 8, pass_same)

        def pass_other(k):
            remote(
                cache1.at[yk(k), :, pl.ds(pl.multiple_of(other * 32, 32), 32), :], cache2.at[y * 2 + c],
                c2, 0, y=yk(k), c=other,
            ).start()

        loop(0, 8, pass_other)
        keep.wait()

    def close_cache():
        sent(most(cache1, 7), c1)
        sent(most(cache2, 15), c2)

        @pl.when(jnp.logical_not(stays))
        def _():
            sent(wkv_v.at[pl.ds(0, 64)], kvsem)

    finals.append(close_cache)

    finish = dp_to_tensor(
        ga, gaz, gax, project, lambda n: part[n, :, c].reshape(32, 384), bcs, bcr, bys, byr, bc, by, cache_pass
    )

    acc = finish()
    factor = lax.rsqrt((acc[:, 320:321] + acc[:, 321:322]) / width + EPS)
    cs[...] = (acc * factor).astype(BF16).astype(F32).reshape(4, 8, 384)

    def share(src, dst, sems):
        def one(n):
            j, to_c = n // 2, lax.rem(c + n % 2, 2)
            remote(src.at[xk(j)], dst.at[x * 2 + c], sems, 0, x=xk(j), c=to_c).start()

        dst[x * 2 + c] = src[x]
        loop(1, 8, one)
        arrived(most(dst, 7), sems, 0)
        finals.append(lambda: sent(most(dst, 7), sems))

    share(cs, cr, csem)

    def rotated(rows):
        count = rows.shape[0] // 16
        cos = jnp.concatenate([rope[0]] * count, axis=0)
        sin = jnp.concatenate([rope[1]] * count, axis=0)
        return (rows * cos + pltpu.roll(rows, 64, 1) * sin).astype(BF16)

    heads = [cr[2 * n : 2 * n + 2].reshape(16, 384) for n in range(4)]
    queries = rotated(
        jnp.concatenate([h[:, a : a + HD] for h in heads for a in (0, HD)], axis=0)
    )
    low = iota((16, HD), 1) < 64
    join = lambda a, b: jnp.where(low, a[:, 256:384], pltpu.roll(b[:, 256:384], 64, 1))
    new_keys = rotated(join(heads[0], heads[1]))
    new_values = join(heads[2], heads[3]).astype(BF16)

    spot = x * 8 + y
    pairs = jnp.concatenate(
        [new_keys, new_values, local_row[...], jnp.zeros((80, HD), BF16)], axis=0
    )
    ds_[:, :, 0:HD] = dot(select[...], queries).astype(BF16).reshape(32, 16, HD)
    ds_[:, :, HD : 2 * HD] = dot(select[...], pairs).astype(BF16).reshape(32, 16, HD)
    dr[spot] = ds_[spot]

    def trade(src, dst, sems):
        def one(n):
            px, py = xk(n // 8), yk(n % 8)
            remote(src.at[px * 8 + py], dst.at[spot], sems, 0, x=px, y=py).start()

        loop(1, 32, one)
        finals.append(lambda: sent(most(src, 31), sems))

    def traded(dst, sems):
        arrived(most(dst, 31), sems, 0)

    trade(ds_, dr, dsem)
    arrived(most(cache2, 15), c2, 0)
    traded(dr, dsem)

    tail = dr[:, :, HD : 2 * HD].astype(F32).reshape(64, 8, HD)
    every_head = lambda n: jnp.broadcast_to(tail[:, n : n + 1, :], (64, 8, HD)).reshape(512, HD)
    own_key, own_value = every_head(0), every_head(1)
    which = jnp.concatenate([every_head(2)[:, 0:1], (iota((128, 1), 0) % 4).astype(F32)], axis=0)
    asked = jnp.concatenate([dr[:, :, 0:HD].reshape(512, HD), queries], axis=0)
    pad = jnp.zeros((112, HD), BF16)
    keys = jnp.concatenate([cache2[:, 0].reshape(512, HD), new_keys, pad], axis=0)
    values = jnp.concatenate([cache2[:, 1].reshape(512, HD), new_values, pad], axis=0)
    scale = 1.0 / math.sqrt(HD)
    scores = lax.dot_general(asked, keys, (((1,), (1,)), ((), ())), preferred_element_type=F32)
    k = iota((1, 640), 1)
    new = k - 512
    key_particle = jnp.where(k < 512, (k // 8) % 4, k % 4)
    key_ok = (k < 512) | ((new < 16) & ((new // 4) % 2 == 0) & (new // 8 == c))
    key_particle = jnp.where(key_ok, key_particle, -1).astype(F32)
    scores = jnp.where(key_particle == which, scores * scale, LOW)
    own = jnp.sum(asked[0:512].astype(F32) * own_key, axis=1, keepdims=True) * scale
    own = jnp.concatenate([own, jnp.full((128, 1), LOW, F32)], axis=0)
    highest = jnp.maximum(jnp.max(scores, axis=1, keepdims=True), own)
    weights = jnp.exp(scores - highest)
    own = jnp.exp(own - highest)
    totals = jnp.sum(weights, axis=1, keepdims=True) + own
    mixed = dot(weights.astype(BF16), values)
    extra = jnp.concatenate([own[0:512] * own_value, jnp.zeros((128, HD), F32)], axis=0)
    mixed = (mixed + extra) / totals

    rs[...] = mixed[0:512].astype(BF16).reshape(32, 16, HD)
    rr[spot] = rs[spot]
    trade(rs, rr, rsem)
    r = iota((128, 1), 0)
    first = jnp.where(((r // 4) % 2 == 0) & ((r // 8) % 2 == c), mixed[512:640], 0.0)
    traded(rr, rsem)
    both = (first + dot(select_t[...], rr[...].reshape(512, HD))).astype(BF16)
    for n in range(4):
        es[n, :, 0:HD] = both[n * 32 : n * 32 + 16]
        es[n, :, HD : 2 * HD] = both[n * 32 + 16 : n * 32 + 32]
    share(es, er, esem)
    for n in range(4):
        mb[y, n * 16 : n * 16 + 16, :] = (er[2 * n].astype(F32) + er[2 * n + 1].astype(F32)).astype(BF16)


    def rows_out(i):
        k = turn(i, z)
        remote(mb.at[y], mb.at[y], e2sem, k, y=yk(k)).start()

    loop(1, 8, rows_out)
    finals.append(lambda: sent(most(mb, 7), e2sem))
    loads[1].wait()

    def rows_came(i, k, n):
        pl.when(i > 0)(lambda: arrived(mb.at[n], e2sem, k))

    attn = tensor_to_dp(
        rows_came, lambda n: dot(mb[n], wo_v[...]), fxs, fxr, fzs, fzr, fx, fz
    ).astype(BF16)
    gg[x, z] = (xrow[...].astype(F32) + attn.astype(F32)).astype(BF16)

    gather_begin(gg, ggz, ggx)

    def give(out, block):
        turned = dot(back16, block)
        out[0] = turned[0:8].astype(BF16)
        out[1] = turned[8:16].astype(BF16)

    give(attn_out, attn)
    loads[2].wait()
    loads[3].wait()

    def gate_up(n):
        away = gg[pl.ds(2 * (1 - c), 2), n].reshape(32, 512)
        here = gg[pl.ds(2 * c, 2), n].reshape(32, 512)
        wide = jnp.concatenate([away, here], axis=0).astype(F32)
        scaled = (wide * ffn_gain[...]).astype(BF16)
        value = dot_t(scaled, wgu_v[...])
        mid = value[:, 384:512] + squares_of(wide)
        hcs[n] = value[0:32].astype(BF16)
        hcs[n, :, 384:512] = mid[0:32].astype(BF16)
        hown[n] = value[32:64]
        hown[n, :, 384:512] = mid[32:64]

    acc = dp_to_tensor(
        gg, ggz, ggx, gate_up, lambda n: hown[n], hcs, hcr, hys, hyr, hc, hy
    )()
    factor = lax.rsqrt((acc[:, ff : ff + 1] + acc[:, ff + 1 : ff + 2]) / width + EPS)
    gate, up = acc[:, 0:512] * factor, acc[:, 512:1024] * factor
    hidden = gate / (1.0 + jnp.exp(-gate)) * up
    hid[c, y] = jnp.where(iota((32, 512), 1) < ff, hidden, 0.0).astype(BF16)

    remote(hid.at[c, y], hid.at[c, y], h2c, 0, c=1 - c).start()

    def hidden_out(i):
        k = turn(i, z)
        remote(hid.at[c, y], hid.at[c, y], h2y, k, y=yk(k)).start()

    loop(1, 8, hidden_out)
    loads[4].wait()

    def pass_hidden(i):
        k = turn(i, z)
        block = hid.at[c, yb(k)]
        arrived(block, h2y, k)
        remote(block, block, h2c, k, c=1 - c).start()

    def hidden_came(i, k, n):
        pl.when(i < 7)(lambda: pass_hidden(i + 1))
        arrived(hid.at[1 - c, n], h2c, k)

    ffn = tensor_to_dp(
        hidden_came, lambda n: dot(hid[:, n].reshape(64, 512), wd_v[...]), ixs, ixr, izs, izr, ix, iz
    )
    give(ffn_out, ffn.astype(BF16))

    sent(hid.at[0, pl.ds(0, 7)], h2y)
    sent(hid.at[0], h2c)
    for close in finals:
        close()


def local(
    x_first, x_second, cache_keys, cache_values, ancestors, attn_gain, ffn_gain,
    w_query, w_keyval, w_out, w_gate, w_up, w_down,
):
    context = cache_keys.shape[1] * NY * NC
    v = lambda *shape: pltpu.VMEM(shape, BF16)
    f = lambda *shape: pltpu.VMEM(shape, F32)
    sem = lambda n: pltpu.SemaphoreType.DMA((2, n))
    near, far = pl.BlockSpec(memory_space=pltpu.VMEM), pl.BlockSpec(memory_space=pl.ANY)
    big = [v(4, 8, 16, 512), v(4, 8, 16, 512), v(8, 16, 512), v(8, 16, 512)]
    return pl.pallas_call(
        kernel,
        out_shape=[jax.ShapeDtypeStruct((2, 8, 512), BF16)] * 2,
        in_specs=[pl.BlockSpec(memory_space=pltpu.SMEM)] + [near] * 5 + [far] * 8,
        out_specs=[near, near],
        scratch_shapes=[
            v(16, 512), v(512, 128), v(128, 512), v(16, HD),
            v(512, 256), v(128, 512), v(256, 512), v(1024, 512), v(512, 512),
            v(4, 8, 16, 512), v(4, 8, 16, 512), f(8, 4, 2, 8, 384),
            *[v(8, 32, 384)] * 4,
            f(4, 8, 384), f(8, 8, 384), v(8, 2, 64, HD), v(16, 2, 32, HD),
            v(32, 16, 256), v(32, 16, 256), v(32, 16, HD), v(32, 16, HD),
            v(4, 16, 256), v(8, 16, 256), v(8, 64, 256),
            *big, *big,
            f(8, 32, 1024), *[v(8, 32, 1024)] * 4, v(2, 8, 32, 512),
            pltpu.SemaphoreType.DMA((8,)), sem(1), sem(8), sem(32), sem(8), sem(32), sem(8), sem(8),
            sem(8), sem(16), sem(16), sem(32), sem(32), sem(8), sem(8),
            sem(32), sem(8), sem(32), sem(8), sem(8), sem(8), sem(8), sem(8),
        ],
        compiler_params=pltpu.CompilerParams(
            collective_id=0, has_side_effects=True, vmem_limit_bytes=VMEM_LIMIT
        ),
        cost_estimate=pl.CostEstimate(flops=2**30, bytes_accessed=2**22, transcendentals=2**19),
    )(
        ancestors, x_first, x_second, attn_gain[None], ffn_gain[None], angles(context),
        cache_keys.reshape(64, -1), cache_values.reshape(64, -1),
        w_query, w_keyval.T, w_out, w_gate.T, w_up.T, w_down,
    )


def solution(mesh):
    fine = Mesh(mesh.devices.reshape(NZ, NX, NY, NC), ("z", "x", "y", "c"))
    rows, cols = P(TENSOR, DP), P(DP, TENSOR)
    return jax.shard_map(
        local,
        mesh=fine,
        in_specs=(
            cols, cols, P(DP, TENSOR, None), P(DP, TENSOR, None), P(), P(TENSOR), P(TENSOR),
            rows, rows, cols, rows, rows, cols,
        ),
        out_specs=(P(None, DP, TENSOR), P(None, DP, TENSOR)),
        check_vma=False,
    )
```

time: 154 us -> 147 us (0.955)
  the two profiles are of different devices: /device:TPU:1 before, /device:TPU:128 now
where the time goes in v3:
time: 147 us
  Pallas kernels  144 us (98%)
  local copies, waits for them, and re-layouts  1.94 us (1%)
    pallas_call x1, Pallas kernels, local(): pl.pallas_call(kernel, out_shape=[jax.ShapeDtypeStruct((2, 8, 512), BF16)...  144 us

profile of v3, /device:TPU:128, one launch (start us, length us, event | category | flops | bytes accessed | tf_op | source)
XLA Modules:
  0.0 146.9 jit_solution(7658118765922071341)
XLA Ops:
  0.6 144.3 %shard_map.149 = (bf16[2,8,512]{2,1,0:T(8,128)(2,1)}, bf16[2,8,512]{2,1,0:T(8,128)(2,1)}) custom-call(s32[256]{0:T(256)} %anc.1, bf16[8,512]{1,0:T(8,128)(2,1)} %x_first.1, bf16[8,512]{1,0:T(8,128)(2,1)} %x_second.1, f32[1,512]{1,0:T(1,128)} %bitcast.12, f32[1,512]{1,0:T(1,128)} %bitcast.13, f32[2,16,128]{2,1,0:T(8,128)} %constant.2.clone.rope, ...), custom_call_target="tpu_custom_call" | custom-call | flops 1073741824 | bytes 4194304 | tf_op jit(solution)/shard_map/pallas_call | solution.py:518
  144.9 0.0 copy-start
  144.9 1.3 copy.18
  146.3 0.0 copy-done
  146.3 0.6 copy.19
Async XLA Ops:
  144.9 1.3 copy-start

commit v4 on v3

--- a/solution.py
+++ b/solution.py
@@ -48,7 +48,7 @@
     ds_, dr, rs, rr, es, er, mb, fxs, fxr, fzs, fzr, ixs, ixr, izs, izr,
     hown, hcs, hcr, hys, hyr, hid,
     lsem, kvsem, gaz, gax, ggz, ggx, bc, by, csem, c1, c2, dsem, rsem, esem, e2sem,
-    fx, fz, ix, iz, hc, hy, h2y, h2c,
+    fx, fz, ix, iz, hc, hy, h2y, h2c, e2c,
 ):
     z, x, y, c = (lax.axis_index(a) for a in ("z", "x", "y", "c"))
     width = x_first.shape[1] * NY * NC
@@ -164,7 +164,7 @@
             remote(csend.at[n], crecv.at[n], cs_, n, c=1 - c).start()
             pl.when(i >= 4)(lambda: to_ring(i - 4))
             if also is not None:
-                pl.when(i == 4)(also)
+                pl.when(i == 2)(also)
 
         pass_on(1)
         loop(0, 8, body)
@@ -424,23 +424,40 @@
         es[n, :, 0:HD] = both[n * 32 : n * 32 + 16]
         es[n, :, HD : 2 * HD] = both[n * 32 + 16 : n * 32 + 32]
     share(es, er, esem)
-    for n in range(4):
-        mb[y, n * 16 : n * 16 + 16, :] = (er[2 * n].astype(F32) + er[2 * n + 1].astype(F32)).astype(BF16)
-
-
-    def rows_out(i):
-        k = turn(i, z)
-        remote(mb.at[y], mb.at[y], e2sem, k, y=yk(k)).start()
-
-    loop(1, 8, rows_out)
-    finals.append(lambda: sent(most(mb, 7), e2sem))
+    for n in range(2):
+        first, second = er[4 * c + 2 * n].astype(F32), er[4 * c + 2 * n + 1].astype(F32)
+        mb[c, y, n * 16 : n * 16 + 16, :] = (first + second).astype(BF16)
+
+    def tensor_begin(buf, ys_, cs_):
+        block = buf.at[c, y]
+        remote(block, block, cs_, 0, c=1 - c).start()
+
+        def one(i):
+            k = turn(i, z)
+            remote(block, block, ys_, k, y=yk(k)).start()
+
+        loop(1, 8, one)
+        finals.append(lambda: sent(buf.at[0, pl.ds(0, 7)], ys_))
+        finals.append(lambda: sent(buf.at[0], cs_))
+
+    def tensor_came(buf, ys_, cs_):
+        def pass_core(i):
+            k = turn(i, z)
+            block = buf.at[c, yb(k)]
+            arrived(block, ys_, k)
+            remote(block, block, cs_, k, c=1 - c).start()
+
+        def came(i, k, n):
+            pl.when(i < 7)(lambda: pass_core(i + 1))
+            arrived(buf.at[1 - c, n], cs_, k)
+
+        return came
+
+    tensor_begin(mb, e2sem, e2c)
     loads[1].wait()
 
-    def rows_came(i, k, n):
-        pl.when(i > 0)(lambda: arrived(mb.at[n], e2sem, k))
-
     attn = tensor_to_dp(
-        rows_came, lambda n: dot(mb[n], wo_v[...]), fxs, fxr, fzs, fzr, fx, fz
+        tensor_came(mb, e2sem, e2c), lambda n: dot(mb[:, n].reshape(64, 256), wo_v[...]), fxs, fxr, fzs, fzr, fx, fz
     ).astype(BF16)
     gg[x, z] = (xrow[...].astype(F32) + attn.astype(F32)).astype(BF16)
 
@@ -475,32 +492,14 @@
     hidden = gate / (1.0 + jnp.exp(-gate)) * up
     hid[c, y] = jnp.where(iota((32, 512), 1) < ff, hidden, 0.0).astype(BF16)
 
-    remote(hid.at[c, y], hid.at[c, y], h2c, 0, c=1 - c).start()
-
-    def hidden_out(i):
-        k = turn(i, z)
-        remote(hid.at[c, y], hid.at[c, y], h2y, k, y=yk(k)).start()
-
-    loop(1, 8, hidden_out)
+    tensor_begin(hid, h2y, h2c)
     loads[4].wait()
 
-    def pass_hidden(i):
-        k = turn(i, z)
-        block = hid.at[c, yb(k)]
-        arrived(block, h2y, k)
-        remote(block, block, h2c, k, c=1 - c).start()
-
-    def hidden_came(i, k, n):
-        pl.when(i < 7)(lambda: pass_hidden(i + 1))
-        arrived(hid.at[1 - c, n], h2c, k)
-
     ffn = tensor_to_dp(
-        hidden_came, lambda n: dot(hid[:, n].reshape(64, 512), wd_v[...]), ixs, ixr, izs, izr, ix, iz
+        tensor_came(hid, h2y, h2c), lambda n: dot(hid[:, n].reshape(64, 512), wd_v[...]), ixs, ixr, izs, izr, ix, iz
     )
     give(ffn_out, ffn.astype(BF16))
 
-    sent(hid.at[0, pl.ds(0, 7)], h2y)
-    sent(hid.at[0], h2c)
     for close in finals:
         close()
 
@@ -527,12 +526,12 @@
             *[v(8, 32, 384)] * 4,
             f(4, 8, 384), f(8, 8, 384), v(8, 2, 64, HD), v(16, 2, 32, HD),
             v(32, 16, 256), v(32, 16, 256), v(32, 16, HD), v(32, 16, HD),
-            v(4, 16, 256), v(8, 16, 256), v(8, 64, 256),
+            v(4, 16, 256), v(8, 16, 256), v(2, 8, 32, 256),
             *big, *big,
             f(8, 32, 1024), *[v(8, 32, 1024)] * 4, v(2, 8, 32, 512),
             pltpu.SemaphoreType.DMA((8,)), sem(1), sem(8), sem(32), sem(8), sem(32), sem(8), sem(8),
             sem(8), sem(16), sem(16), sem(32), sem(32), sem(8), sem(8),
-            sem(32), sem(8), sem(32), sem(8), sem(8), sem(8), sem(8), sem(8),
+            sem(32), sem(8), sem(32), sem(8), sem(8), sem(8), sem(8), sem(8), sem(8),
         ],
         compiler_params=pltpu.CompilerParams(
             collective_id=0, has_side_effects=True, vmem_limit_bytes=VMEM_LIMIT

time: 147 us -> 144 us (0.980)
  the two profiles are of different devices: /device:TPU:128 before, /device:TPU:1 now
where the time goes in v4:
time: 144 us; the launch traced here: 142 us
  Pallas kernels  140 us (97%)
  local copies, waits for them, and re-layouts  1.94 us (1%)
    pallas_call x1, Pallas kernels, local(): pl.pallas_call(kernel, out_shape=[jax.ShapeDtypeStruct((2, 8, 512), BF16)...  140 us

profile of v4, /device:TPU:1, one launch (start us, length us, event | category | flops | bytes accessed | tf_op | source)
XLA Modules:
  0.0 142.1 jit_solution(8359517956851351609)
XLA Ops:
  0.6 139.5 %shard_map.149 = (bf16[2,8,512]{2,1,0:T(8,128)(2,1)}, bf16[2,8,512]{2,1,0:T(8,128)(2,1)}) custom-call(s32[256]{0:T(256)} %anc.1, bf16[8,512]{1,0:T(8,128)(2,1)} %x_first.1, bf16[8,512]{1,0:T(8,128)(2,1)} %x_second.1, f32[1,512]{1,0:T(1,128)} %bitcast.12, f32[1,512]{1,0:T(1,128)} %bitcast.13, f32[2,16,128]{2,1,0:T(8,128)} %constant.2.clone.rope, ...), custom_call_target="tpu_custom_call" | custom-call | flops 1073741824 | bytes 4194304 | tf_op jit(solution)/shard_map/pallas_call | solution.py:517
  140.2 0.0 copy-start
  140.2 1.3 copy.18
  141.5 0.0 copy-done
  141.5 0.6 copy.19
Async XLA Ops:
  140.2 1.3 copy-start
